TPU v7x, 128 devices: a whole 4x4x4 slice. The times are simulated.
128 devices in a mesh: shape: 8 (over z, core), grp: 16 (over y, x).
Axes of the slice: x: 4, y: 4, z: 4, core: 2. Of those that a mesh axis runs over, the one named last changes fastest.
Arguments:
- latents: bfloat16 [512, 64, 64, 128], P(('shape', 'grp')), parts along dimension 0, may hold values from -6 to 6
- up_weight: bfloat16 [3, 3, 3, 128, 64], replicated, may hold values from -0.25 to 0.25
- first_weight: bfloat16 [3, 3, 3, 64, 64], replicated, may hold values from -0.15625 to 0.15625
- second_weight: bfloat16 [3, 3, 3, 64, 64], replicated, may hold values from -0.15625 to 0.15625
- brick_ids: int32 [2048], P(('shape', 'grp')), parts along dimension 0, may hold values from -1 to 255, as said below
- brick_owner: int32 [2048], P(('shape', 'grp')), parts along dimension 0, may hold values from -1 to 15, as said below
- neighbor_live: int32 [2048, 27], P(('shape', 'grp')), parts along dimension 0, may hold values 0 or 1
Outputs:
- fine_bricks: bfloat16 [4096, 32768], P(('shape', 'grp')), parts along dimension 0
There are 8 independent parts, one for each index of `shape`. A program takes and returns all parts, laid end to end along the dimension named above; an argument that names none is the same for every part. Nothing has to cross between parts.
Inputs may be any that keep to these rules, and one draw needn't show every extreme that they name: `brick_ids`: each device's block of 16 entries lists distinct bricks of its own panel by local number (x slowest, z fastest), -1 for an unused entry; every block uses 16 - 16 // 2 to 16 entries at any positions, and some block uses all of them. `brick_owner`: -1 exactly where brick_ids is -1. Within one device's block no owner appears more than 2 times among used entries, and one owner appears exactly 2 times among the used entries of every block.
All inputs are finite; a program needn't handle non-finite values. No bound on the sum of `neighbor_live` on one device may be relied on, other than what follows from the above.
Results may differ from a plain program's by a relative error of at most 0.0052.
Values may be sent and summed in bfloat16 or wider, within the bound.
A program may use at most 128 MiB of HBM per device.

v0:
```python
import jax
import jax.numpy as jnp
from jax import lax
from jax.sharding import PartitionSpec as P

BE = 8
HB = 4
G = 64
PX = 4


parity_taps = (((1, 0),), ((2, 0), (0, 1)))


def extended_2(block, sides, width):
    for axis, dim in sides:
        count = lax.axis_size(axis)
        forward = [(i, i + 1) for i in range(count - 1)]
        backward = [(target, source) for source, target in forward]
        low = lax.ppermute(
            lax.slice_in_dim(block, block.shape[dim] - width, None, axis=dim), axis, forward
        )
        high = lax.ppermute(lax.slice_in_dim(block, 0, width, axis=dim), axis, backward)
        block = jnp.concatenate([low, block, high], axis=dim)
    return block


def upsample(regions, weight):
    sub_edge = regions.shape[1] - 1
    parity_grids = []
    for parity_x in range(2):
        plane_list = []
        for parity_y in range(2):
            line_list = []
            for parity_z in range(2):
                pieces = []
                kernels = []
                for tap_x, shift_x in parity_taps[parity_x]:
                    for tap_y, shift_y in parity_taps[parity_y]:
                        for tap_z, shift_z in parity_taps[parity_z]:
                            pieces.append(
                                regions[
                                    :,
                                    shift_x : shift_x + sub_edge,
                                    shift_y : shift_y + sub_edge,
                                    shift_z : shift_z + sub_edge,
                                    :,
                                ]
                            )
                            kernels.append(weight[tap_x, tap_y, tap_z])
                stacked = jnp.concatenate(pieces, axis=-1)
                kernel = jnp.concatenate(kernels, axis=0)
                line_list.append(
                    jnp.einsum(
                        "bxyzc,co->bxyzo", stacked, kernel, preferred_element_type=jnp.float32
                    )
                )
            plane_list.append(jnp.stack(line_list, axis=4))
        parity_grids.append(jnp.stack(plane_list, axis=3))
    alternated = jnp.stack(parity_grids, axis=2)
    return alternated.reshape(
        regions.shape[0], 2 * sub_edge, 2 * sub_edge, 2 * sub_edge, weight.shape[-1]
    )


def cell_mask(live_flags, full_edge):
    cell_pos = jnp.arange(full_edge, dtype=jnp.int32)
    neighbor_class = (cell_pos >= 2).astype(jnp.int32) + (cell_pos >= full_edge - 2).astype(
        jnp.int32
    )
    selector = (neighbor_class[:, None] == jnp.arange(3, dtype=jnp.int32)[None, :]).astype(
        jnp.float32
    )
    flag_cube = live_flags.reshape(live_flags.shape[0], 3, 3, 3)
    return jnp.einsum("bijk,xi,yj,zk->bxyz", flag_cube, selector, selector, selector)


def conv_valid(inputs, kernel):
    return lax.conv_general_dilated(
        inputs,
        kernel,
        (1, 1, 1),
        "VALID",
        dimension_numbers=("NDHWC", "DHWIO", "NDHWC"),
        preferred_element_type=jnp.float32,
    )


def refine(extended, full_mask, first_weight, second_weight):
    first_out = conv_valid(extended, first_weight)
    hidden = (jax.nn.silu(first_out) * full_mask[:, 1:-1, 1:-1, 1:-1, None]).astype(jnp.bfloat16)
    second_out = conv_valid(hidden, second_weight)
    refined = extended[:, 2:-2, 2:-2, 2:-2, :].astype(jnp.float32) + second_out
    return refined.astype(jnp.bfloat16).reshape(extended.shape[0], -1)


def neighbor_flags(brick_x, brick_y, brick_z, in_use, neighbor_live, bricks_long, bricks_across):
    offsets = jnp.arange(27, dtype=jnp.int32)
    step_x = offsets // 9 - 1
    step_y = offsets // 3 % 3 - 1
    step_z = offsets % 3 - 1
    near_x = brick_x[:, None] + step_x[None, :]
    near_y = brick_y[:, None] + step_y[None, :]
    near_z = brick_z[:, None] + step_z[None, :]
    inside = (
        (near_x >= 0)
        & (near_x < bricks_long)
        & (near_y >= 0)
        & (near_y < bricks_across)
        & (near_z >= 0)
        & (near_z < bricks_across)
    )
    chosen = (neighbor_live > 0) | (offsets == 13)[None, :]
    return (inside & chosen & in_use[:, None]).astype(jnp.float32)


def local(latents, up_weight, first_weight, second_weight, brick_ids, brick_owner, neighbor_live):
    group_size = lax.axis_size("grp")
    device_pos = lax.axis_index("grp")
    listed = brick_ids.shape[0]
    capacity = max(2, listed // group_size)
    slot_count = group_size * capacity
    across = G // HB
    panel_bricks = PX // HB
    channels = latents.shape[3]
    full_edge = BE + 4
    in_use = brick_ids >= 0
    safe_ids = jnp.maximum(brick_ids, 0)
    local_x = safe_ids // (across * across)
    brick_y = safe_ids // across % across
    brick_z = safe_ids % across
    rimmed = extended_2(latents, (("grp", 0),), 2)
    padded = jnp.pad(rimmed, ((0, 0), (1, 2), (1, 2), (0, 0)))

    def slice_region(start_x, start_y, start_z):
        starts = (start_x * HB + 1, start_y * HB, start_z * HB, jnp.int32(0))
        return lax.dynamic_slice(padded, starts, (HB + 3, HB + 3, HB + 3, channels))

    regions = jax.vmap(slice_region)(local_x, brick_y, brick_z)
    brick_x = device_pos * panel_bricks + local_x
    live_flags = neighbor_flags(
        brick_x, brick_y, brick_z, in_use, neighbor_live, panel_bricks * group_size, across
    )
    full_mask = cell_mask(live_flags, full_edge)
    extended = (upsample(regions, up_weight) * full_mask[..., None]).astype(jnp.bfloat16)
    owner_onehot = (
        (brick_owner[:, None] == jnp.arange(group_size, dtype=jnp.int32)[None, :]) & in_use[:, None]
    ).astype(jnp.int32)
    earlier = jnp.cumsum(owner_onehot, axis=0) - owner_onehot
    owner_rank = jnp.sum(earlier * owner_onehot, axis=1)
    target = jnp.where(in_use, brick_owner * capacity + owner_rank, slot_count)
    refined = refine(extended, full_mask, first_weight, second_weight)
    out_rows = (
        jnp.zeros((slot_count, refined.shape[1]), jnp.bfloat16).at[target].set(refined, mode="drop")
    )
    return lax.all_to_all(out_rows, "grp", split_axis=0, concat_axis=0, tiled=True)


def solution(mesh):
    in_specs = (
        P(("shape", "grp"), None, None, None),
        P(),
        P(),
        P(),
        P(("shape", "grp")),
        P(("shape", "grp")),
        P(("shape", "grp"), None),
    )
    out_specs = P(("shape", "grp"), None)
    return jax.shard_map(local, mesh=mesh, in_specs=in_specs, out_specs=out_specs, check_vma=False)
```

profile of v0, /device:TPU:0, one launch (start us, length us, event | category | flops | bytes accessed | tf_op | source)
XLA Modules:
  0.0 416.4 jit_solution(1835799462238331103)
XLA Ops:
  0.0 5.3 %fusion.103 = (bf16[2,64,64,128]{3,2,1,0:T(8,128)(2,1)}, bf16[2,64,64,128]{3,2,1,0:T(8,128)(2,1)}) fusion(bf16[4,64,64,128]{3,2,1,0:T(8,128)(2,1)} %param.7), kind=kLoop, calls=%fused_computation.196 | loop fusion | bytes 8388608 | tf_op jit(solution)/shard_map/slice | solution.py:21
  5.3 4.8 %collective-permute-start = (bf16[2,64,64,128]{3,2,1,0:T(8,128)(2,1)}, bf16[2,64,64,128]{3,2,1,0:T(8,128)(2,1)}, u32[]{:S(2)}, u32[]{:S(2)}) collective-permute-start(bf16[2,64,64,128]{3,2,1,0:T(8,128)(2,1)} %get-tuple-element.30), channel_id=1, source_target_pairs={{0,1},{1,2},{2,3},{3,4},{4,5},{5,6},{6,7},{7,8},{8,9},{9,10},{10,1... | collective-permute-start | bytes 6291464 | tf_op jit(solution)/shard_map/ppermute | solution.py:20
  10.1 1.3 collective-permute-start.1
  13.1 0.9 copy.28
  14.0 1.2 slice.203
  15.2 2.7 copy.29
  18.1 35.9 %collective-permute-done = bf16[2,64,64,128]{3,2,1,0:T(8,128)(2,1)} collective-permute-done((bf16[2,64,64,128]{3,2,1,0:T(8,128)(2,1)}, bf16[2,64,64,128]{3,2,1,0:T(8,128)(2,1)}, u32[]{:S(2)}, u32[]{:S(2)}) %collective-permute-start) | collective-permute-done | bytes 2097184 | tf_op jit(solution)/shard_map/ppermute | solution.py:20
  53.9 5.5 %collective-permute-done.1 = bf16[2,64,64,128]{3,2,1,0:T(8,128)(2,1)} collective-permute-done((bf16[2,64,64,128]{3,2,1,0:T(8,128)(2,1)}, bf16[2,64,64,128]{3,2,1,0:T(8,128)(2,1)}, u32[]{:S(2)}, u32[]{:S(2)}) %collective-permute-start.1) | collective-permute-done | bytes 2097184 | tf_op jit(solution)/shard_map/ppermute | solution.py:23
  59.4 12.4 %select_maximum_fusion = bf16[8,67,67,128]{3,2,1,0:T(8,128)(2,1)} fusion(bf16[2,64,64,128]{3,2,1,0:T(8,128)(2,1)} %collective-permute-done.1, bf16[4,64,64,128]{3,2,1,0:T(8,128)(2,1)} %param.7, bf16[2,64,64,128]{3,2,1,0:T(8,128)(2,1)} %collective-permute-done), kind=kLoop, calls=%fused_computation.12 | loop fusion | flops 87337984 | bytes 17582080 | tf_op jit(solution)/shard_map/concatenate | solution.py:24
  71.8 66.5 %while.1 = (s32[]{:T(128)}, bf16[8,67,67,128]{3,2,1,0:T(8,128)(2,1)}, s32[16,4]{0,1:T(4,128)S(1)}, bf16[16,7,7,7,128]{4,3,2,1,0:T(8,128)(2,1)}, s32[]{:T(128)}) while((s32[]{:T(128)}, bf16[8,67,67,128]{3,2,1,0:T(8,128)(2,1)}, s32[16,4]{0,1:T(4,128)S(1)}, bf16[16,7,7,7,128]{4,3,2,1,0:T(8,128)(2,1)}, s32[]{:T(128)}) %tuple.56), condition=%wide.while_cond, body=%wide.while_body.sunk | while | flops 2 | bytes 202873 | solution.py:137
  71.8 0.5 fusion.112
  72.4 3.5 bitcast_dynamic-update-slice_fusion.2
  76.0 0.5 fusion.112
  76.5 3.5 bitcast_dynamic-update-slice_fusion.2
  80.1 0.5 fusion.112
  80.7 3.5 bitcast_dynamic-update-slice_fusion.2
  84.3 0.5 fusion.112
  84.8 3.5 bitcast_dynamic-update-slice_fusion.2
  88.4 0.5 fusion.112
  88.9 3.5 bitcast_dynamic-update-slice_fusion.2
  92.5 0.5 fusion.112
  93.1 3.5 bitcast_dynamic-update-slice_fusion.2
  96.7 0.5 fusion.112
  97.2 3.5 bitcast_dynamic-update-slice_fusion.2
  100.8 0.5 fusion.112
  101.4 3.5 bitcast_dynamic-update-slice_fusion.2
  104.9 0.5 fusion.112
  105.5 3.5 bitcast_dynamic-update-slice_fusion.2
  109.1 0.5 fusion.112
  109.7 3.5 bitcast_dynamic-update-slice_fusion.2
  113.3 0.5 fusion.112
  113.8 3.5 bitcast_dynamic-update-slice_fusion.2
  117.4 0.5 fusion.112
  117.9 3.5 bitcast_dynamic-update-slice_fusion.2
  121.5 0.5 fusion.112
  122.1 3.5 bitcast_dynamic-update-slice_fusion.2
  126.2 3.5 bitcast_dynamic-update-slice_fusion.2
  130.4 3.5 bitcast_dynamic-update-slice_fusion.2
  134.5 3.5 bitcast_dynamic-update-slice_fusion.2
  138.3 1.6 copy.18
  139.9 2.4 fusion.104
  145.7 0.6 fusion.28
  146.3 0.6 fusion.29
  146.9 1.1 fusion.30
  148.0 1.1 maximum_bitcast_fusion.2
  149.1 3.9 maximum_bitcast_fusion
  153.0 2.0 convolution_bitcast_fusion.1
  155.0 0.6 fusion.27
  155.6 0.6 copy-done.3
  156.1 1.1 fusion.33
  157.3 1.1 fusion.36
  158.4 1.3 maximum_bitcast_fusion.4
  159.6 3.7 maximum_bitcast_fusion.1
  163.3 12.9 %pad_maximum_fusion = f32[16,6,2,6,2,6,2,64]{7,0,5,3,1,6,4,2:T(8,128)} fusion(f32[16,6,1,6,2,6,2,64]{7,0,5,3,1,6,4,2:T(8,128)} %maximum_bitcast_fusion.1, f32[16,6,1,6,2,6,2,64]{7,0,5,3,1,6,4,2:T(8,128)} %maximum_bitcast_fusion), kind=kLoop, calls=%fused_computation.10 | loop fusion | flops 1769472 | bytes 14155776 | tf_op jit(solution)/shard_map/stack | solution.py:60
  176.2 12.1 %copy.26 = f32[16,6,2,6,2,6,2,64]{7,0,6,5,4,3,2,1:T(8,128)} copy(f32[16,6,2,6,2,6,2,64]{7,0,5,3,1,6,4,2:T(8,128)} %pad_maximum_fusion) | data formatting | bytes 14155776 | tf_op jit(solution)/shard_map/stack | solution.py:60
  188.3 8.2 %multiply_convert_fusion = bf16[16,12,12,12,64]{4,0,3,2,1:T(8,128)(2,1)S(1)} fusion(f32[16,12,12,12,64]{4,0,3,2,1:T(8,128)} %bitcast.161, f32[16,12,12,12]{0,3,2,1:T(8,128)S(1)} %copy.28), kind=kLoop, calls=%fused_computation.11 | loop fusion | flops 3538944 | bytes 10727424 | tf_op jit(solution)/shard_map/convert_element_type | solution.py:145
  196.5 163.8 %fusion.105 = f32[16,10,10,10,64]{4,0,3,2,1:T(8,128)S(1)} fusion(bf16[16,12,12,12,64]{4,0,3,2,1:T(8,128)(2,1)S(1)} %multiply_convert_fusion, bf16[3,3,3,64,64]{4,3,2,1,0:T(8,128)(2,1)S(1)} %copy-done), kind=kOutput, calls=%fused_computation.198 | convolution fusion | flops 3538944000 | bytes 7856128 | tf_op jit(solution)/shard_map/conv_general_dilated | solution.py:79
  360.3 9.2 %add_convert_fusion = bf16[16,8,8,8,64]{4,0,3,2,1:T(8,128)(2,1)S(1)} fusion(bf16[16,12,12,12,64]{4,0,3,2,1:T(8,128)(2,1)S(1)} %multiply_convert_fusion, bf16[3,3,3,64,64]{4,3,2,1,0:T(8,128)(2,1)S(1)} %copy-done.9, f32[16,10,10,10,64]{4,0,3,2,1:T(8,128)S(1)} %fusion.105, f32[16,10,10,10]{0,3,2,1:T(8,128)S(1)} %copy-done.4), kind=kOutput, calls=%fused_computation.24 | convolution fusion | flops 1819656192 | bytes 6478336 | tf_op jit(solution)/shard_map/conv_general_dilated | solution.py:79
  369.5 0.6 copy.30
  370.0 2.5 reshape.104
  372.5 3.5 scatter_custom_fusion
  376.1 2.6 all_to_all.8
  378.7 35.3 %all_to_all.12 = bf16[16,2,32768]{2,1,0:T(2,128)(2,1)S(1)} all-to-all(bf16[16,2,32768]{2,1,0:T(2,128)(2,1)} %all_to_all.8), channel_id=1, replica_groups=mesh['shape'=8,'grp'=16] {'grp'}, dimensions={0} | all-to-all | bytes 4194304 | tf_op jit(solution)/shard_map/all_to_all | solution.py:156
  414.0 2.2 all_to_all.10
  (74 shorter events, 7.9 us)
Async XLA Ops:
  0.0 196.5 %copy-start = (bf16[3,3,3,64,64]{4,3,2,1,0:T(8,128)(2,1)S(1)}, bf16[3,3,3,64,64]{4,3,2,1,0:T(8,128)(2,1)}, u32[]{:S(2)}) copy-start(bf16[3,3,3,64,64]{4,3,2,1,0:T(8,128)(2,1)} %param.9) | copy-start | bytes 663556
  0.0 11.5 %copy-start.8 = (s32[16]{0:T(128)S(1)}, s32[16]{0:T(128)}, u32[]{:S(2)}) copy-start(s32[16]{0:T(128)} %param.11) | copy-start | bytes 196
  0.0 11.5 %copy-start.7 = (s32[16]{0:T(128)S(1)}, s32[16]{0:T(128)}, u32[]{:S(2)}) copy-start(s32[16]{0:T(128)} %param.12) | copy-start | bytes 196
  0.0 11.9 %copy-start.6 = (s32[16,27]{1,0:T(8,128)S(1)}, s32[16,27]{1,0:T(8,128)}, u32[]{:S(2)}) copy-start(s32[16,27]{1,0:T(8,128)} %param.13) | copy-start | bytes 5188
  5.3 48.7 %collective-permute-start = (bf16[2,64,64,128]{3,2,1,0:T(8,128)(2,1)}, bf16[2,64,64,128]{3,2,1,0:T(8,128)(2,1)}, u32[]{:S(2)}, u32[]{:S(2)}) collective-permute-start(bf16[2,64,64,128]{3,2,1,0:T(8,128)(2,1)} %get-tuple-element.30), channel_id=1, source_target_pairs={{0,1},{1,2},{2,3},{3,4},{4,5},{5,6},{6,7},{7,8},{8,9},{9,10},{10,1... | collective-permute-start | bytes 6291464 | tf_op jit(solution)/shard_map/ppermute | solution.py:20
  10.1 49.3 %collective-permute-start.1 = (bf16[2,64,64,128]{3,2,1,0:T(8,128)(2,1)}, bf16[2,64,64,128]{3,2,1,0:T(8,128)(2,1)}, u32[]{:S(2)}, u32[]{:S(2)}) collective-permute-start(bf16[2,64,64,128]{3,2,1,0:T(8,128)(2,1)} %get-tuple-element.31), channel_id=1, source_target_pairs={{1,0},{2,1},{3,2},{4,3},{5,4},{6,5},{7,6},{8,7},{9,8},{10,9},{11,1... | collective-permute-start | bytes 6291464 | tf_op jit(solution)/shard_map/ppermute | solution.py:23
  12.3 5.6 %copy-start.5 = (bf16[3,3,3,128,64]{3,4,2,1,0:T(8,128)(2,1)S(1)}, bf16[3,3,3,128,64]{3,4,2,1,0:T(8,128)(2,1)}, u32[]{:S(2)}) copy-start(bf16[3,3,3,128,64]{3,4,2,1,0:T(8,128)(2,1)} %param.8) | copy-start | bytes 1327108
  155.0 1.2 copy-start.3
  156.1 1.2 copy-start.2
  196.5 163.8 %copy-start.4 = (f32[16,10,10,10]{0,3,2,1:T(8,128)S(1)}, f32[16,10,10,10]{0,3,2,1:T(8,128)}, u32[]{:S(2)}) copy-start(f32[16,10,10,10]{0,3,2,1:T(8,128)} %copy.29) | copy-start | bytes 192004
  196.5 163.8 %copy-start.9 = (bf16[3,3,3,64,64]{4,3,2,1,0:T(8,128)(2,1)S(1)}, bf16[3,3,3,64,64]{4,3,2,1,0:T(8,128)(2,1)}, u32[]{:S(2)}) copy-start(bf16[3,3,3,64,64]{4,3,2,1,0:T(8,128)(2,1)} %param.10) | copy-start | bytes 663556
  376.1 40.1 %copy-start.1 = (bf16[3,3,3,64,64]{4,3,2,1,0:T(8,128)(2,1)S(1)}, bf16[3,3,3,64,64]{4,3,2,1,0:T(8,128)(2,1)}, u32[]{:S(2)}) copy-start(bf16[3,3,3,64,64]{4,3,2,1,0:T(8,128)(2,1)} %param.9) | copy-start | bytes 663556
where the time goes:
time: 422 us; the launch traced here: 416 us
  matrix products  181 us (43%)
  local copies, waits for them, and re-layouts  108 us (26%)
  other arithmetic  43.9 us (10%)
  waiting for transfers between devices  41.3 us (10%)
  blocking collectives  35.3 us (8%)
  starting transfers between devices  6.13 us (1%)
    conv_general_dilated x2, matrix products, conv_valid(): lax.conv_general_dilated(inputs, kernel, (1, 1, 1), 'VALID', dimension_nu...  173 us
    gather x48, local copies, waits for them, and re-layouts  66.2 us
    ppermute x1, waiting for transfers between devices, extended_2(): lax.ppermute(lax.slice_in_dim(block, block.shape[dim] - width, None, axis...  35.9 us
    all_to_all x1, blocking collectives, local(): lax.all_to_all(out_rows, 'grp', split_axis=0, concat_axis=0, tiled=True)  35.3 us
    another operation x3, other arithmetic, upsample(): alternated = jnp.stack(parity_grids, axis=2)  20.5 us
    concatenate x1, other arithmetic, extended_2(): block = jnp.concatenate([low, block, high], axis=dim)  12.4 us
    another operation x1, local copies, waits for them, and re-layouts, upsample(): alternated = jnp.stack(parity_grids, axis=2)  12.1 us
  transfers between devices with their start and end apart: 2, of which 2 were waited for; matrix products, arithmetic and copies ran while one was open for 2% of the time, Pallas kernels for 0%

commit v1 on v0

v1 whole, which is shorter than its diff:
```python
import jax
import jax.numpy as jnp
from jax import lax
from jax.experimental import pallas as pl
from jax.experimental.pallas import tpu as pltpu
from jax.sharding import PartitionSpec as P

G = 64
HB = 4
NB = 16
VMEM = pltpu.VMEM
SMEM = pltpu.SMEM
F32 = jnp.float32
BF16 = jnp.bfloat16


def conv_weights(w):
    z = jnp.zeros_like(w[:, :, :1])
    a = jnp.concatenate([jnp.concatenate([w, z], 2), jnp.concatenate([z, w], 2)], -1)
    z = jnp.zeros_like(a[:, :1])
    b = jnp.concatenate([jnp.concatenate([a, z], 1), jnp.concatenate([z, a], 1)], -1)
    return b.reshape(3, 1024, 256)


def up_weights(w):
    z = jnp.zeros_like(w[:, :, 0])
    a = jnp.stack(
        [jnp.concatenate([w[:, :, 1], w[:, :, 2]], -1), jnp.concatenate([z, w[:, :, 0]], -1)], 2
    )
    z = jnp.zeros_like(a[:, 0])
    b = jnp.stack(
        [jnp.concatenate([a[:, 1], a[:, 2]], -1), jnp.concatenate([z, a[:, 0]], -1)], 1
    )
    return b.reshape(3, 512, 256)


def gather_kernel(own_ids, prev_ids, next_ids, lat_ref, own_ref, down_ref, up_ref, pan, win):
    plane = pl.program_id(0)

    @pl.when(plane == 0)
    def _():
        pan[0] = jnp.zeros(pan.shape[1:], F32)
        pan[65:67] = jnp.zeros((2,) + pan.shape[1:], F32)
        pan[:, 0:8] = jnp.zeros((67, 8, 128), F32)
        pan[:, 72:80] = jnp.zeros((67, 8, 128), F32)

    pan[1:65, 8:72] = lat_ref[0].astype(F32)

    def gather(ids, out_ref):
        for b in range(NB):
            local = jnp.maximum(ids[b], 0)
            by = lax.rem(lax.div(local, 16), 16)
            bz = lax.rem(local, 16)
            for j in range(7):
                win[pl.ds((j * NB + b) * 8, 8), :] = pan[4 * by + j, pl.ds(4 * bz + 7, 8), :]
        for j in range(7):
            for l in range(7):
                out_ref[0, j, l] = win[pl.ds(j * 128 + l, 16, stride=8), :].astype(BF16)

    gather(own_ids, own_ref)

    @pl.when(plane < 2)
    def _():
        gather(prev_ids, down_ref)

    @pl.when(plane == 3)
    def _():
        gather(next_ids, up_ref)


def gather_regions(latents, own_ids, prev_ids, next_ids):
    smem = pl.BlockSpec(memory_space=SMEM)
    block = (1, 7, 7, NB, 128)
    return pl.pallas_call(
        gather_kernel,
        grid=(4,),
        in_specs=[smem, smem, smem, pl.BlockSpec((1, G, G, 128), lambda i: (i, 0, 0, 0))],
        out_specs=[
            pl.BlockSpec(block, lambda i: (i, 0, 0, 0, 0)),
            pl.BlockSpec(block, lambda i: (jnp.minimum(i, 1), 0, 0, 0, 0)),
            pl.BlockSpec(block, lambda i: (0, 0, 0, 0, 0)),
        ],
        out_shape=[
            jax.ShapeDtypeStruct((4, 7, 7, NB, 128), BF16),
            jax.ShapeDtypeStruct((2, 7, 7, NB, 128), BF16),
            jax.ShapeDtypeStruct((1, 7, 7, NB, 128), BF16),
        ],
        scratch_shapes=[VMEM((67, 80, 128), F32), VMEM((7 * NB * 8, 128), F32)],
        compiler_params=pltpu.CompilerParams(vmem_limit_bytes=32 << 20),
        name="gather_regions",
    )(own_ids, prev_ids, next_ids, latents)


def refine_kernel(
    inv, low_ref, own_ref, high_ref, live_ref, wu_ref, w1_ref, w2_ref, out_ref, reg, ext, hid, emask, hmask, fin
):
    reg[0:1] = low_ref[...]
    reg[1:5] = own_ref[...]
    reg[5:7] = high_ref[...]

    for n in range(27):
        emask[n // 9, n // 3 % 3, n % 3] = jnp.broadcast_to(live_ref[:, n : n + 1], (NB, 128))
    first = lax.broadcasted_iota(jnp.int32, (NB, 128), 1) < 64
    pair = ((0, 1), (1, 1), (1, 2))
    for cx in range(3):
        for cy in range(3):
            for cz in range(3):
                for py in range(2):
                    za, zb = pair[cz]
                    hmask[cx, cy, cz, py] = jnp.where(
                        first, emask[cx, pair[cy][py], za], emask[cx, pair[cy][py], zb]
                    )

    def spread(m, n):
        m = jnp.concatenate([m[0:1]] + [m[1:2]] * (n - 2) + [m[2:3]], 0)
        return jnp.concatenate([m[:, 0:1]] + [m[:, 1:2]] * (n - 2) + [m[:, 2:3]], 1)

    def dot(a, b):
        return jnp.dot(a, b, preferred_element_type=F32)

    def up_step(sub, _):
        def patch(i):
            return jnp.concatenate(
                [
                    reg[i, sy : sy + 6, sz : sz + 6].reshape(36 * NB, 128)
                    for sy in range(2)
                    for sz in range(2)
                ],
                1,
            )

        here, after = patch(sub), patch(sub + 1)
        even = dot(here, wu_ref[1])
        odd = dot(here, wu_ref[2]) + dot(after, wu_ref[0])
        cx = (sub >= 1).astype(jnp.int32) + (sub >= 5).astype(jnp.int32)
        m = spread(emask[cx], 6)
        for p, value in ((0, even), (1, odd)):
            for h in range(2):
                part = value[:, h * 128 : h * 128 + 128].reshape(6, 6, NB, 128)
                ext[2 * sub + p, :, :, h] = (part * m).astype(BF16)
        return 0

    lax.fori_loop(0, 6, up_step, 0)

    def conv(src, x, n, w_ref):
        total = None
        for kx in range(3):
            patch = jnp.concatenate(
                [
                    src[x + kx, dy : dy + n, dz : dz + n, qy].reshape(n * n * NB, 128)
                    for dy in range(2)
                    for qy in range(2)
                    for dz in range(2)
                ],
                1,
            )
            term = dot(patch, w_ref[kx])
            total = term if total is None else total + term
        return total

    def first_step(x, _):
        v = conv(ext, x, 5, w1_ref)
        v = (0.5 * v) * (1.0 + jnp.tanh(0.5 * v))
        cx = (x >= 1).astype(jnp.int32) + (x >= 9).astype(jnp.int32)
        m = hmask[cx]
        for h in range(2):
            part = v[:, h * 128 : h * 128 + 128].reshape(5, 5, NB, 128)
            hid[x, :, :, h] = (part * spread(m[:, :, h], 5)).astype(BF16)
        return 0

    lax.fori_loop(0, 10, first_step, 0)

    def second_step(x, _):
        v = conv(hid, x, 4, w2_ref)
        for py in range(2):
            part = v[:, py * 128 : py * 128 + 128].reshape(4, 4, NB, 128)
            part = part + ext[x + 2, 1:5, 1:5, py].astype(F32)
            for cy in range(4):
                fin[pl.ds((2 * cy + py) * 4 * NB, 4 * NB), :] = part[cy].reshape(4 * NB, 128)
        for s in range(32):
            b = jnp.maximum(inv[s], 0)
            used = inv[s] >= 0
            for g in range(2):
                rows = fin[pl.ds(g * 256 + b, 16, stride=NB), :]
                out_ref[s, pl.ds(pl.multiple_of(x * 32 + g * 16, 16), 16), :] = jnp.where(used, rows, 0.0).astype(BF16)
        return 0

    lax.fori_loop(0, 8, second_step, 0)


def refine_slots(inv, low, own, high, live, wu, w1, w2):
    vmem = pl.BlockSpec(memory_space=VMEM)
    return pl.pallas_call(
        refine_kernel,
        in_specs=[pl.BlockSpec(memory_space=SMEM)] + [vmem] * 7,
        out_specs=vmem,
        out_shape=jax.ShapeDtypeStruct((32, 256, 128), BF16),
        scratch_shapes=[
            VMEM((7, 7, 7, NB, 128), BF16),
            VMEM((12, 6, 6, 2, NB, 128), BF16),
            VMEM((10, 5, 5, 2, NB, 128), BF16),
            VMEM((3, 3, 3, NB, 128), F32),
            VMEM((3, 3, 3, 2, NB, 128), F32),
            VMEM((32 * NB, 128), F32),
        ],
        compiler_params=pltpu.CompilerParams(vmem_limit_bytes=48 << 20),
        name="refine_slots",
    )(inv, low, own, high, live, wu, w1, w2)


def live_flags(ids, neighbor_live, bricks_long, bricks_across):
    used = ids >= 0
    local = jnp.maximum(ids, 0)
    n = jnp.arange(27, dtype=jnp.int32)
    near_x = (lax.axis_index("grp") + local // (bricks_across * bricks_across))[:, None] + n // 9 - 1
    near_y = (local // bricks_across % bricks_across)[:, None] + n // 3 % 3 - 1
    near_z = (local % bricks_across)[:, None] + n % 3 - 1
    inside = (near_x >= 0) & (near_x < bricks_long)
    inside &= (near_y >= 0) & (near_y < bricks_across)
    inside &= (near_z >= 0) & (near_z < bricks_across)
    return (inside & ((neighbor_live > 0) | (n == 13)) & used[:, None]).astype(F32)


def slot_sources(ids, owner):
    used = ids >= 0
    r = jnp.arange(NB, dtype=jnp.int32)
    same = (owner[:, None] == owner[None, :]) & used[None, :] & (r[None, :] < r[:, None])
    slot = jnp.where(used, owner * 2 + jnp.sum(same.astype(jnp.int32), 1), -1)
    hit = slot[:, None] == jnp.arange(32, dtype=jnp.int32)[None, :]
    return jnp.sum(jnp.where(hit, r[:, None] + 1, 0), 0) - 1


def local(latents, up_weight, first_weight, second_weight, brick_ids, brick_owner, neighbor_live):
    count = lax.axis_size("grp")
    up = [(i, i + 1) for i in range(count - 1)]
    down = [(i + 1, i) for i in range(count - 1)]
    prev_ids = lax.ppermute(brick_ids, "grp", up)
    next_ids = lax.ppermute(brick_ids, "grp", down)
    own, to_prev, to_next = gather_regions(latents, brick_ids, prev_ids, next_ids)
    low = lax.ppermute(to_next, "grp", up)
    high = lax.ppermute(to_prev, "grp", down)
    live = live_flags(brick_ids, neighbor_live, count, G // HB)
    inv = slot_sources(brick_ids, brick_owner)
    slots = refine_slots(
        inv, low, own, high, live, up_weights(up_weight), conv_weights(first_weight), conv_weights(second_weight)
    )
    rows = lax.all_to_all(slots, "grp", split_axis=0, concat_axis=0, tiled=True)
    return rows.reshape(32, 32768)


def solution(mesh):
    rows = P(("shape", "grp"))
    in_specs = (rows, P(), P(), P(), rows, rows, rows)
    return jax.shard_map(local, mesh=mesh, in_specs=in_specs, out_specs=rows, check_vma=False)
```

time: 422 us -> 91 us (0.22); the launches traced: 416 us -> 90.4 us
  matrix products: 181 us -> 0 us
  local copies, waits for them, and re-layouts: 108 us -> 6.69 us
  waiting for transfers between devices: 41.3 us -> 1.73 us
  other arithmetic: 43.9 us -> 6.69 us
  Pallas kernels: 0 us -> 24.5 us
  starting transfers between devices: 6.13 us -> 11.8 us
    conv_general_dilated x2 -> x0, matrix products: 173 us -> none  [conv_valid(): lax.conv_general_dilated(inputs, kernel, (1, 1, 1), 'VALID', dimension_nu...]
    gather x49 -> x0, local copies, waits for them, and re-layouts: 67.9 us -> none
    ppermute x2 -> x4, waiting for transfers between devices: 41.3 us -> 1.73 us  [the longest x1 1.73 us: local(): high = lax.ppermute(to_prev, 'grp', down)]
    pallas_call x0 -> x2, Pallas kernels: none -> 24.5 us  [the longest x1 21.4 us: refine_slots(): pl.pallas_call(refine_kernel, in_specs=[pl.BlockSpec(memory_space=SMEM)]...]
    another operation x6 -> x3, other arithmetic: 22.9 us -> 1.03 us  [the longest x2 0.98 us: up_weights(): jnp.stack([jnp.concatenate([a[:, 1], a[:, 2]], -1), jnp.concatenate([z, a...]
    slice x4 -> x0, local copies, waits for them, and re-layouts: 11.6 us -> none  [the longest x1 5.25 us: extended_2(): lax.slice_in_dim(block, block.shape[dim] - width, None, axis=dim)]
    another operation x1 -> x2, local copies, waits for them, and re-layouts: 12.1 us -> 1.44 us  [up_weights(): jnp.stack([jnp.concatenate([a[:, 1], a[:, 2]], -1), jnp.concatenate([z, a...]
    concatenate x2 -> x4, other arithmetic: 12.4 us -> 3.11 us  [the longest x2 1.64 us: conv_weights(): jnp.concatenate([jnp.concatenate([a, z], 1), jnp.concatenate([z, a], 1)],...]
  transfers between devices with their start and end apart: 2 -> 4, of which waited for: 2 -> 1; matrix products, arithmetic and copies ran while one was open for 2% -> 10% of each run, Pallas kernels for 0% -> 0%
where the time goes in v1:
time: 91 us; the launch traced here: 90.4 us
  blocking collectives  38.9 us (43%)
  Pallas kernels  24.5 us (27%)
  starting transfers between devices  11.8 us (13%)
  other arithmetic  6.69 us (7%)
  local copies, waits for them, and re-layouts  6.69 us (7%)
  waiting for transfers between devices  1.73 us (2%)
    all_to_all x1, blocking collectives, local(): rows = lax.all_to_all(slots, 'grp', split_axis=0, concat_axis=0, tiled=True)  38.9 us
    pallas_call x1, Pallas kernels, refine_slots(): pl.pallas_call(refine_kernel, in_specs=[pl.BlockSpec(memory_space=SMEM)]...  21.4 us
    ppermute x1, starting transfers between devices, local(): prev_ids = lax.ppermute(brick_ids, 'grp', up)  4.55 us
    ppermute x1, starting transfers between devices, local(): low = lax.ppermute(to_next, 'grp', up)  4.55 us
    unnamed x11, local copies, waits for them, and re-layouts  4.15 us
    pallas_call x1, Pallas kernels, gather_regions(): pl.pallas_call(gather_kernel, grid=(4,), in_specs=[smem, smem, smem, pl.B...  3.06 us
  transfers between devices with their start and end apart: 4, of which 1 were waited for; matrix products, arithmetic and copies ran while one was open for 10% of the time, Pallas kernels for 0%

profile of v1, /device:TPU:0, one launch (start us, length us, event | category | flops | bytes accessed | tf_op | source)
XLA Modules:
  0.0 90.4 jit_solution(5793454765159851284)
XLA Ops:
  0.0 1.3 %collective-permute-start.1 = (s32[16]{0:T(128)}, s32[16]{0:T(128)S(1)}, u32[]{:S(2)}, u32[]{:S(2)}) collective-permute-start(s32[16]{0:T(128)} %own_ids.1), channel_id=1, source_target_pairs={{1,0},{2,1},{3,2},{4,3},{5,4},{6,5},{7,6},{8,7},{9,8},{10,9},{11,1... | collective-permute-start | bytes 200 | tf_op jit(solution)/shard_map/ppermute | solution.py:238
  1.3 4.6 %collective-permute-start = (s32[16]{0:T(128)}, s32[16]{0:T(128)S(1)}, u32[]{:S(2)}, u32[]{:S(2)}) collective-permute-start(s32[16]{0:T(128)} %own_ids.1), channel_id=1, source_target_pairs={{0,1},{1,2},{2,3},{3,4},{4,5},{5,6},{6,7},{7,8},{8,9},{9,10},{10,1... | collective-permute-start | bytes 200 | tf_op jit(solution)/shard_map/ppermute | solution.py:237
  5.9 0.7 broadcast_compare_fusion
  6.6 0.9 %convert_reduce_fusion = s32[16]{0:T(128)S(1)} fusion(s32[16]{0:T(128)} %param.12, pred[16]{0:T(512)(128)(4,1)S(1)} %broadcast_compare_fusion), kind=kLoop, calls=%fused_computation.46 | loop fusion | flops 1520 | bytes 144 | tf_op jit(solution)/shard_map/reduce_sum | solution.py:228
  7.5 0.7 fusion.34
  8.2 0.1 select_reduce_fusion
  8.3 1.1 %slice_bitcast_fusion.2 = (bf16[3,3,128,64]{2,3,1,0:T(8,128)(2,1)S(1)}, bf16[3,3,128,64]{2,3,1,0:T(8,128)(2,1)S(1)}, bf16[3,3,128,64]{2,3,1,0:T(8,128)(2,1)S(1)}) fusion(bf16[3,3,3,128,64]{3,4,2,1,0:T(8,128)(2,1)} %param.8), kind=kLoop, calls=%fused_computation.34 | loop fusion | bytes 884736 | tf_op jit(solution)/shard_map/squeeze | solution.py:28
  9.4 0.0 copy-start.2
  9.4 0.1 maximum_bitcast_fusion.1
  9.4 0.0 copy-start.4
  9.5 0.1 fusion.15
  9.5 0.0 copy-start
  9.6 0.8 copy-done.2
  10.4 0.3 fusion.11
  10.7 0.0 copy-start.1
  10.7 0.2 fusion.5
  10.9 0.0 copy-done.4
  10.9 0.1 fusion.30.live_ref
  11.1 0.0 collective-permute-done.1.next_ids
  11.1 0.0 collective-permute-done.prev_ids
  11.1 0.7 copy-done
  11.7 0.0 copy-done.1
  11.7 3.1 %gather_regions.1 = (bf16[4,7,7,16,128]{4,3,2,1,0:T(8,128)(2,1)S(1)}, bf16[2,7,7,16,128]{4,3,2,1,0:T(8,128)(2,1)}, bf16[1,7,7,16,128]{4,3,2,1,0:T(8,128)(2,1)}) custom-call(s32[16]{0:T(128)S(1)} %copy-done.1, s32[16]{0:T(128)S(1)} %collective-permute-done.prev_ids, s32[16]{0:T(128)S(1)} %collective-permute-done.1.next_ids, bf16[4,64,64,128]{3,2,1,0:T(8,128)(2,1)S(1)} %copy-done), custom_call_target="tpu_custom_call" | custom-call | tf_op jit(solution)/shard_map/gather_regions/pallas_call | solution.py:74
  14.8 0.0 copy-start.3
  14.8 1.4 %collective-permute-start.3 = (bf16[2,7,7,16,128]{4,3,2,1,0:T(8,128)(2,1)}, bf16[2,7,7,16,128]{4,3,2,1,0:T(8,128)(2,1)}, u32[]{:S(2)}, u32[]{:S(2)}) collective-permute-start(bf16[2,7,7,16,128]{4,3,2,1,0:T(8,128)(2,1)} %get-tuple-element.10), channel_id=1, source_target_pairs={{1,0},{2,1},{3,2},{4,3},{5,4},{6,5},{7,6},{8,7},{9,8},{10,9},{11,1... | collective-permute-start | bytes 1204232 | tf_op jit(solution)/shard_map/ppermute | solution.py:241
  16.2 0.9 %pad_maximum_fusion = bf16[3,2,2,128,256]{3,4,0,2,1:T(8,128)(2,1)} fusion(bf16[3,1,2,128,256]{3,4,0,2,1:T(8,128)(2,1)S(1)} %pad_bitcast_fusion, bf16[3,1,2,128,256]{3,4,0,2,1:T(8,128)(2,1)S(1)} %maximum_bitcast_fusion), kind=kLoop, calls=%fused_computation.15 | loop fusion | flops 393216 | bytes 1572864 | tf_op jit(solution)/shard_map/stack | solution.py:31
  17.2 4.5 %collective-permute-start.2 = (bf16[1,7,7,16,128]{4,3,2,1,0:T(8,128)(2,1)}, bf16[1,7,7,16,128]{4,3,2,1,0:T(8,128)(2,1)S(1)}, u32[]{:S(2)}, u32[]{:S(2)}) collective-permute-start(bf16[1,7,7,16,128]{4,3,2,1,0:T(8,128)(2,1)} %get-tuple-element.8), channel_id=1, source_target_pairs={{0,1},{1,2},{2,3},{3,4},{4,5},{5,6},{6,7},{7,8},{8,9},{9,10},{10,1... | collective-permute-start | bytes 602120 | tf_op jit(solution)/shard_map/ppermute | solution.py:240
  21.7 0.0 copy-done.3
  21.7 1.1 %fusion.10 = bf16[3,3,4,64,128]{4,3,2,1,0:T(8,128)(2,1)} fusion(bf16[3,3,3,64,64]{4,3,2,1,0:T(8,128)(2,1)S(1)} %copy-done.3), kind=kLoop, calls=%fused_computation.20 | loop fusion | flops 2359296 | bytes 811008 | tf_op jit(solution)/shard_map/concatenate | solution.py:19
  22.9 1.4 %copy.17 = bf16[3,2,2,128,256]{4,3,2,1,0:T(8,128)(2,1)S(1)} copy(bf16[3,2,2,128,256]{3,4,0,2,1:T(8,128)(2,1)} %pad_maximum_fusion) | data formatting | bytes 1572864 | tf_op jit(solution)/shard_map/stack | solution.py:31
  24.3 1.4 %fusion.4 = bf16[3,4,4,64,256]{4,3,2,1,0:T(8,128)(2,1)S(1)} fusion(bf16[3,3,4,64,128]{4,3,2,1,0:T(8,128)(2,1)} %fusion.10), kind=kLoop, calls=%fused_computation.7 | loop fusion | flops 6291456 | bytes 2162688 | tf_op jit(solution)/shard_map/concatenate | solution.py:21
  25.7 0.0 collective-permute-done.2.low_ref
  25.7 1.7 %collective-permute-done.3.high_ref = bf16[2,7,7,16,128]{4,3,2,1,0:T(8,128)(2,1)} collective-permute-done((bf16[2,7,7,16,128]{4,3,2,1,0:T(8,128)(2,1)}, bf16[2,7,7,16,128]{4,3,2,1,0:T(8,128)(2,1)}, u32[]{:S(2)}, u32[]{:S(2)}) %collective-permute-start.3) | collective-permute-done | bytes 401440 | tf_op jit(solution)/shard_map/ppermute | solution.py:241
  27.5 21.4 %refine_slots.1 = bf16[32,256,128]{2,1,0:T(8,128)(2,1)} custom-call(s32[32]{0:T(128)S(1)} %broadcast_add_fusion.inv, bf16[1,7,7,16,128]{4,3,2,1,0:T(8,128)(2,1)S(1)} %collective-permute-done.2.low_ref, bf16[4,7,7,16,128]{4,3,2,1,0:T(8,128)(2,1)S(1)} %get-tuple-element.9.own_ref, bf16[2,7,7,16,128]{4,3,2,1,0:T(8,128)(2,1)} %collective-permute-done.3.high_ref, ...), custom_call_target="tpu_custom_call" | custom-call | tf_op jit(solution)/shard_map/refine_slots/pallas_call | solution.py:193
  48.9 38.9 %all_to_all.5 = bf16[32,256,128]{2,1,0:T(8,128)(2,1)S(1)} all-to-all(bf16[32,256,128]{2,1,0:T(8,128)(2,1)} %refine_slots.1), channel_id=1, replica_groups=mesh['shape'=8,'grp'=16] {'grp'}, dimensions={0} | all-to-all | bytes 4194304 | tf_op jit(solution)/shard_map/all_to_all | solution.py:247
  87.8 2.7 %copy.24 = bf16[4,8,256,128]{3,1,2,0:T(8,128)(2,1)} copy(bf16[4,8,256,128]{3,2,1,0:T(8,128)(2,1)S(1)} %bitcast.38) | data formatting | bytes 4194304
  (7 shorter events, 0.1 us)
Async XLA Ops:
  0.0 11.1 %collective-permute-start.1 = (s32[16]{0:T(128)}, s32[16]{0:T(128)S(1)}, u32[]{:S(2)}, u32[]{:S(2)}) collective-permute-start(s32[16]{0:T(128)} %own_ids.1), channel_id=1, source_target_pairs={{1,0},{2,1},{3,2},{4,3},{5,4},{6,5},{7,6},{8,7},{9,8},{10,9},{11,1... | collective-permute-start | bytes 200 | tf_op jit(solution)/shard_map/ppermute | solution.py:238
  1.3 9.8 %collective-permute-start = (s32[16]{0:T(128)}, s32[16]{0:T(128)S(1)}, u32[]{:S(2)}, u32[]{:S(2)}) collective-permute-start(s32[16]{0:T(128)} %own_ids.1), channel_id=1, source_target_pairs={{0,1},{1,2},{2,3},{3,4},{4,5},{5,6},{6,7},{7,8},{8,9},{9,10},{10,1... | collective-permute-start | bytes 200 | tf_op jit(solution)/shard_map/ppermute | solution.py:237
  9.4 1.0 %copy-start.2 = (bf16[3,3,3,64,64]{4,3,2,1,0:T(8,128)(2,1)S(1)}, bf16[3,3,3,64,64]{4,3,2,1,0:T(8,128)(2,1)}, u32[]{:S(2)}) copy-start(bf16[3,3,3,64,64]{4,3,2,1,0:T(8,128)(2,1)} %param.10) | copy-start | bytes 663556
  9.4 1.5 %copy-start.4 = (s32[16,27]{1,0:T(8,128)S(1)}, s32[16,27]{1,0:T(8,128)}, u32[]{:S(2)}) copy-start(s32[16,27]{1,0:T(8,128)} %param.13) | copy-start | bytes 5188
  9.5 2.2 %copy-start = (bf16[4,64,64,128]{3,2,1,0:T(8,128)(2,1)S(1)}, bf16[4,64,64,128]{3,2,1,0:T(8,128)(2,1)}, u32[]{:S(2)}) copy-start(bf16[4,64,64,128]{3,2,1,0:T(8,128)(2,1)} %lat_ref.1) | copy-start | bytes 12582916
  10.7 1.0 %copy-start.1 = (s32[16]{0:T(128)S(1)}, s32[16]{0:T(128)}, u32[]{:S(2)}) copy-start(s32[16]{0:T(128)} %own_ids.1) | copy-start | bytes 196
  14.8 6.9 %copy-start.3 = (bf16[3,3,3,64,64]{4,3,2,1,0:T(8,128)(2,1)S(1)}, bf16[3,3,3,64,64]{4,3,2,1,0:T(8,128)(2,1)}, u32[]{:S(2)}) copy-start(bf16[3,3,3,64,64]{4,3,2,1,0:T(8,128)(2,1)} %param.9) | copy-start | bytes 663556
  14.8 12.7 %collective-permute-start.3 = (bf16[2,7,7,16,128]{4,3,2,1,0:T(8,128)(2,1)}, bf16[2,7,7,16,128]{4,3,2,1,0:T(8,128)(2,1)}, u32[]{:S(2)}, u32[]{:S(2)}) collective-permute-start(bf16[2,7,7,16,128]{4,3,2,1,0:T(8,128)(2,1)} %get-tuple-element.10), channel_id=1, source_target_pairs={{1,0},{2,1},{3,2},{4,3},{5,4},{6,5},{7,6},{8,7},{9,8},{10,9},{11,1... | collective-permute-start | bytes 1204232 | tf_op jit(solution)/shard_map/ppermute | solution.py:241
  17.2 8.6 %collective-permute-start.2 = (bf16[1,7,7,16,128]{4,3,2,1,0:T(8,128)(2,1)}, bf16[1,7,7,16,128]{4,3,2,1,0:T(8,128)(2,1)S(1)}, u32[]{:S(2)}, u32[]{:S(2)}) collective-permute-start(bf16[1,7,7,16,128]{4,3,2,1,0:T(8,128)(2,1)} %get-tuple-element.8), channel_id=1, source_target_pairs={{0,1},{1,2},{2,3},{3,4},{4,5},{5,6},{6,7},{7,8},{8,9},{9,10},{10,1... | collective-permute-start | bytes 602120 | tf_op jit(solution)/shard_map/ppermute | solution.py:240

commit v2 on v1

v2 whole, which is shorter than its diff:
```python
import jax
import jax.numpy as jnp
from jax import lax
from jax.experimental import pallas as pl
from jax.experimental.pallas import tpu as pltpu
from jax.sharding import PartitionSpec as P

G = 64
HB = 4
NB = 16
VMEM = pltpu.VMEM
SMEM = pltpu.SMEM
DMA = pltpu.SemaphoreType.DMA
F32 = jnp.float32
BF16 = jnp.bfloat16
MESH = pl.DeviceIdType.MESH

PEERS = sorted(
    ((dy, dx) for dy in range(4) for dx in range(4) if dy or dx),
    key=lambda s: -(min(s[0], 4 - s[0]) + min(s[1], 4 - s[1])),
)
UP_TAP = ((1, 2), (None, 0))
PHASES = (
    ((2, 5), (2, 7), ((1, 0), (1, 1), (2, 0), (2, 1), (3, 0), (3, 1), (4, 0))),
    ((0, 2), (0, 2), ((0, 0), (0, 1))),
    ((5, 8), (7, 10), ((4, 1), (5, 0), (5, 1))),
)


def kernel(
    ids,
    owner,
    lat_hbm,
    wu_hbm,
    w1_hbm,
    w2_hbm,
    near_ref,
    out_ref,
    lat,
    wu_raw,
    w1_raw,
    w2_raw,
    wu,
    w1,
    w2,
    pan,
    win,
    reg,
    to_prev,
    to_next,
    ext,
    hid,
    emask,
    hmask,
    fin,
    send,
    near_ids,
    inv,
    lat_sem,
    w_sem,
    id_send,
    id_recv,
    halo_send,
    halo_recv,
    own_sem,
    send_sem,
    recv_sem,
):
    count = lax.axis_size("grp")
    me = lax.axis_index("grp")
    row, col = me // 4, me % 4
    across = G // HB

    def peer(dy, dx):
        return (row + dy) % 4 * 4 + (col + dx) % 4

    barrier = pltpu.get_barrier_semaphore()
    for dy, dx in PEERS:
        pl.semaphore_signal(barrier, inc=1, device_id={"grp": peer(dy, dx)}, device_id_type=MESH)

    def lat_copy(p):
        return pltpu.make_async_copy(lat_hbm.at[p], lat.at[p], lat_sem.at[p])

    for p in range(4):
        lat_copy(p).start()
    w_copies = [
        pltpu.make_async_copy(s, d, w_sem.at[i])
        for i, (s, d) in enumerate(((wu_hbm, wu_raw), (w1_hbm, w1_raw), (w2_hbm, w2_raw)))
    ]
    for c in w_copies:
        c.start()

    slot = []
    for b in range(NB):
        rank = 0
        for r in range(b):
            rank = rank + jnp.where(owner[r] == owner[b], 1, 0)
        slot.append(jnp.where(ids[b] >= 0, owner[b] * 2 + rank, -1))
    for s in range(32):
        source = -1
        for b in range(NB):
            source = jnp.where(slot[b] == s, b, source)
        inv[s] = source

    entry = lax.broadcasted_iota(jnp.int32, (NB, 27), 0)
    n = lax.broadcasted_iota(jnp.int32, (NB, 27), 1)
    local = jnp.full((NB, 27), -1, jnp.int32)
    for b in range(NB):
        local = jnp.where(entry == b, ids[b], local)
    used = local >= 0
    local = jnp.maximum(local, 0)
    near_x = me + local // (across * across) + n // 9 - 1
    near_y = local // across % across + n // 3 % 3 - 1
    near_z = local % across + n % 3 - 1
    inside = (near_x >= 0) & (near_x < count) & (near_y >= 0) & (near_y < across)
    inside = inside & (near_z >= 0) & (near_z < across)
    live = jnp.where(inside & ((near_ref[...] > 0) | (n == 13)) & used, 1.0, 0.0)
    for k in range(27):
        emask[k // 9, k // 3 % 3, k % 3] = jnp.broadcast_to(live[:, k : k + 1], (NB, 128))
    first = lax.broadcasted_iota(jnp.int32, (NB, 128), 1) < 64
    pair = ((0, 1), (1, 1), (1, 2))
    for cx in range(3):
        for cy in range(3):
            for cz in range(3):
                for py in range(2):
                    za, zb = pair[cz]
                    hmask[cx, cy, cz, py] = jnp.where(
                        first, emask[cx, pair[cy][py], za], emask[cx, pair[cy][py], zb]
                    )

    pl.semaphore_wait(barrier, len(PEERS))
    id_up = pltpu.make_async_remote_copy(
        ids, near_ids.at[0], id_send.at[0], id_recv.at[0], device_id={"grp": me + 1}, device_id_type=MESH
    )
    id_down = pltpu.make_async_remote_copy(
        ids, near_ids.at[1], id_send.at[1], id_recv.at[1], device_id={"grp": me - 1}, device_id_type=MESH
    )

    @pl.when(me < count - 1)
    def _():
        id_up.start()

    @pl.when(me > 0)
    def _():
        id_down.start()

    def border(p, _):
        pan[p, 0] = jnp.zeros(pan.shape[2:], F32)
        pan[p, 65:67] = jnp.zeros((2,) + pan.shape[2:], F32)
        pan[p, :, 0:8] = jnp.zeros((67, 8, 128), F32)
        pan[p, :, 72:80] = jnp.zeros((67, 8, 128), F32)
        return 0

    lax.fori_loop(0, 4, border, 0)

    def gather(p, id_of, dst, q):
        def one(b, _):
            local = jnp.maximum(id_of(b), 0)
            by = local // across % across
            bz = local % across
            for j in range(7):
                win[pl.ds(pl.multiple_of((j * NB + b) * 8, 8), 8), :] = pan[p, 4 * by + j, pl.ds(4 * bz + 7, 8), :]
            return 0

        lax.fori_loop(0, NB, one, 0)

        def two(j, _):
            for l in range(7):
                dst[q, j, l] = win[pl.ds(j * 128 + l, NB, stride=8), :].astype(BF16)
            return 0

        lax.fori_loop(0, 7, two, 0)

    def plane_step(p, _):
        lat_copy(p).wait()
        pan[p, 1:65, 8:72] = lat[p].astype(F32)
        gather(p, lambda b: ids[b], reg, p + 1)
        return 0

    lax.fori_loop(0, 4, plane_step, 0)

    halo_up = pltpu.make_async_remote_copy(
        to_next, reg.at[pl.ds(0, 1)], halo_send.at[0], halo_recv.at[0], device_id={"grp": me + 1}, device_id_type=MESH
    )
    halo_down = pltpu.make_async_remote_copy(
        to_prev, reg.at[pl.ds(5, 2)], halo_send.at[1], halo_recv.at[1], device_id={"grp": me - 1}, device_id_type=MESH
    )

    @pl.when(me > 0)
    def _():
        id_up.wait_recv()
        gather(0, lambda b: near_ids[0, b], to_prev, 0)
        gather(1, lambda b: near_ids[0, b], to_prev, 1)
        halo_down.start()

    @pl.when(me < count - 1)
    def _():
        id_down.wait_recv()
        gather(3, lambda b: near_ids[1, b], to_next, 0)
        halo_up.start()

    for c in w_copies:
        c.wait()

    def wu_step(kx, _):
        for sy in range(2):
            for sz in range(2):
                parts = []
                for py in range(2):
                    for pz in range(2):
                        ky, kz = UP_TAP[sy][py], UP_TAP[sz][pz]
                        parts.append(
                            jnp.zeros((128, 64), BF16) if ky is None or kz is None else wu_raw[kx, ky, kz]
                        )
                at = (sy * 2 + sz) * 128
                wu[kx, at : at + 128] = jnp.concatenate(parts, 1)
        return 0

    lax.fori_loop(0, 3, wu_step, 0)

    def patch_weights(src, dst):
        def step(kx, _):
            zero = jnp.zeros((64, 64), BF16)

            def pick(ky, kz):
                return src[kx, ky, kz] if 0 <= ky < 3 and 0 <= kz < 3 else zero

            for ty in range(4):
                for tz in range(4):
                    parts = [pick(ty - py, tz - pz) for py in range(2) for pz in range(2)]
                    at = (ty * 4 + tz) * 64
                    dst[kx, at : at + 64] = jnp.concatenate(parts, 1)
            return 0

        lax.fori_loop(0, 3, step, 0)

    patch_weights(w1_raw, w1)
    patch_weights(w2_raw, w2)

    def spread(m, n):
        m = jnp.concatenate([m[0:1]] + [m[1:2]] * (n - 2) + [m[2:3]], 0)
        return jnp.concatenate([m[:, 0:1]] + [m[:, 1:2]] * (n - 2) + [m[:, 2:3]], 1)

    def dot(a, b):
        return jnp.dot(a, b, preferred_element_type=F32)

    def up_plane(sub, parity):
        def patch(i):
            return jnp.concatenate(
                [
                    reg[i, sy : sy + 6, sz : sz + 6].reshape(36 * NB, 128)
                    for sy in range(2)
                    for sz in range(2)
                ],
                1,
            )

        if parity:
            value = dot(patch(sub), wu[2]) + dot(patch(sub + 1), wu[0])
        else:
            value = dot(patch(sub), wu[1])
        m = spread(emask[(sub >= 1) + (sub >= 5)], 6)
        for h in range(2):
            part = value[:, h * 128 : h * 128 + 128].reshape(6, 6, NB, 128)
            ext[2 * sub + parity, :, :, h] = (part * m).astype(BF16)

    def conv(src, x, n, w_ref):
        total = None
        for kx in range(3):
            patch = jnp.concatenate(
                [
                    src[x + kx, dy : dy + n, dz : dz + n, qy].reshape(n * n * NB, 128)
                    for dy in range(2)
                    for qy in range(2)
                    for dz in range(2)
                ],
                1,
            )
            term = dot(patch, w_ref[kx])
            total = term if total is None else total + term
        return total

    def first_step(x, _):
        v = conv(ext, x, 5, w1)
        v = (0.5 * v) * (1.0 + jnp.tanh(0.5 * v))
        m = hmask[(x >= 1).astype(jnp.int32) + (x >= 9).astype(jnp.int32)]
        for h in range(2):
            part = v[:, h * 128 : h * 128 + 128].reshape(5, 5, NB, 128)
            hid[x, :, :, h] = (part * spread(m[:, :, h], 5)).astype(BF16)
        return 0

    def second_step(x, _):
        v = conv(hid, x, 4, w2)
        for py in range(2):
            part = v[:, py * 128 : py * 128 + 128].reshape(4, 4, NB, 128)
            part = part + ext[x + 2, 1:5, 1:5, py].astype(F32)
            for cy in range(4):
                fin[pl.ds((2 * cy + py) * 4 * NB, 4 * NB), :] = part[cy].reshape(4 * NB, 128)
        for s in range(32):
            b = jnp.maximum(inv[s], 0)
            filled = inv[s] >= 0
            for g in range(2):
                rows = fin[pl.ds(g * 256 + b, NB, stride=NB), :]
                at = pl.multiple_of(x * 32 + g * 16, 16)
                send[s, pl.ds(at, 16), :] = jnp.where(filled, rows, 0.0).astype(BF16)
        return 0

    copies = []
    for phase, ((x0, x1), (h0, h1), planes) in enumerate(PHASES):
        if phase == 1:

            @pl.when(me == 0)
            def _():
                reg[0] = jnp.zeros(reg.shape[1:], BF16)

            @pl.when(me > 0)
            def _():
                halo_up.wait_recv()

        if phase == 2:

            @pl.when(me == count - 1)
            def _():
                reg[5:7] = jnp.zeros((2,) + reg.shape[1:], BF16)

            @pl.when(me < count - 1)
            def _():
                halo_down.wait_recv()

        for sub, parity in planes:
            up_plane(sub, parity)
        lax.fori_loop(h0, h1, first_step, 0)
        lax.fori_loop(x0, x1, second_step, 0)
        cells = pl.ds(x0 * 32, (x1 - x0) * 32)
        own = pltpu.make_async_copy(
            send.at[pl.ds(2 * me, 2), cells], out_ref.at[pl.ds(2 * me, 2), cells], own_sem.at[phase]
        )
        for k, (dy, dx) in enumerate(PEERS):
            to = peer(dy, dx)
            c = pltpu.make_async_remote_copy(
                send.at[pl.ds(2 * to, 2), cells],
                out_ref.at[pl.ds(2 * me, 2), cells],
                send_sem.at[phase, k],
                recv_sem.at[phase, k],
                device_id={"grp": to},
                device_id_type=MESH,
            )
            c.start()
            copies.append(c)
        own.start()
        copies.append(own)

    @pl.when(me < count - 1)
    def _():
        id_up.wait_send()
        halo_up.wait_send()

    @pl.when(me > 0)
    def _():
        id_down.wait_send()
        halo_down.wait_send()

    for c in copies:
        c.wait()


def decode(ids, owner, latents, wu, w1, w2, near):
    smem = pl.BlockSpec(memory_space=SMEM)
    hbm = pl.BlockSpec(memory_space=pl.ANY)
    return pl.pallas_call(
        kernel,
        in_specs=[smem, smem, hbm, hbm, hbm, hbm, pl.BlockSpec(memory_space=VMEM)],
        out_specs=hbm,
        out_shape=jax.ShapeDtypeStruct((32, 256, 128), BF16),
        scratch_shapes=[
            VMEM((4, G, G, 128), BF16),
            VMEM((3, 3, 3, 128, 64), BF16),
            VMEM((3, 3, 3, 64, 64), BF16),
            VMEM((3, 3, 3, 64, 64), BF16),
            VMEM((3, 512, 256), BF16),
            VMEM((3, 1024, 256), BF16),
            VMEM((3, 1024, 256), BF16),
            VMEM((4, 67, 80, 128), F32),
            VMEM((7 * NB * 8, 128), F32),
            VMEM((7, 7, 7, NB, 128), BF16),
            VMEM((2, 7, 7, NB, 128), BF16),
            VMEM((1, 7, 7, NB, 128), BF16),
            VMEM((12, 6, 6, 2, NB, 128), BF16),
            VMEM((10, 5, 5, 2, NB, 128), BF16),
            VMEM((3, 3, 3, NB, 128), F32),
            VMEM((3, 3, 3, 2, NB, 128), F32),
            VMEM((32 * NB, 128), F32),
            VMEM((32, 256, 128), BF16),
            SMEM((2, NB), jnp.int32),
            SMEM((32,), jnp.int32),
            DMA((4,)),
            DMA((3,)),
            DMA((2,)),
            DMA((2,)),
            DMA((2,)),
            DMA((2,)),
            DMA((3,)),
            DMA((3, 15)),
            DMA((3, 15)),
        ],
        compiler_params=pltpu.CompilerParams(
            collective_id=0, has_side_effects=True, vmem_limit_bytes=56 << 20
        ),
        name="decode",
    )(ids, owner, latents, wu, w1, w2, near)


def local(latents, up_weight, first_weight, second_weight, brick_ids, brick_owner, neighbor_live):
    rows = decode(brick_ids, brick_owner, latents, up_weight, first_weight, second_weight, neighbor_live)
    return rows.reshape(32, 32768)


def solution(mesh):
    rows = P(("shape", "grp"))
    in_specs = (rows, P(), P(), P(), rows, rows, rows)
    return jax.shard_map(local, mesh=mesh, in_specs=in_specs, out_specs=rows, check_vma=False)
```

time: 91 us -> 51.9 us (0.57)
  blocking collectives: 38.9 us -> 0 us
  Pallas kernels: 24.5 us -> 44.7 us
  starting transfers between devices: 11.8 us -> 0 us
  other arithmetic: 6.69 us -> 0 us
  waiting for transfers between devices: 1.73 us -> 0 us
    all_to_all x1 -> x0, blocking collectives: 38.9 us -> none  [local(): rows = lax.all_to_all(slots, 'grp', split_axis=0, concat_axis=0, tiled=True)]
    pallas_call x2 -> x1, Pallas kernels: 24.5 us -> 44.7 us  [decode(): pl.pallas_call(kernel, in_specs=[smem, smem, hbm, hbm, hbm, hbm, pl.Block...]
    ppermute x4 -> x0, starting transfers between devices: 11.8 us -> none  [the longest x1 4.55 us: local(): prev_ids = lax.ppermute(brick_ids, 'grp', up)]
    concatenate x4 -> x0, other arithmetic: 3.11 us -> none  [the longest x2 1.64 us: conv_weights(): jnp.concatenate([jnp.concatenate([a, z], 1), jnp.concatenate([z, a], 1)],...]
    unnamed x11 -> x2, local copies, waits for them, and re-layouts: 4.15 us -> 6.5 us
    ppermute x4 -> x0, waiting for transfers between devices: 1.73 us -> none  [the longest x1 1.73 us: local(): high = lax.ppermute(to_prev, 'grp', down)]
    another operation x2 -> x0, local copies, waits for them, and re-layouts: 1.44 us -> none  [up_weights(): jnp.stack([jnp.concatenate([a[:, 1], a[:, 2]], -1), jnp.concatenate([z, a...]
    squeeze x1 -> x0, local copies, waits for them, and re-layouts: 1.09 us -> none  [up_weights(): w[:, :, 1]]
  transfers between devices with their start and end apart: 4 -> 0, of which waited for: 1 -> 0; matrix products, arithmetic and copies ran while one was open for 10% -> 0% of each run, Pallas kernels for 0% -> 0%
where the time goes in v2:
time: 51.9 us; the launch traced here: 51.2 us
  Pallas kernels  44.7 us (86%)
  local copies, waits for them, and re-layouts  6.5 us (13%)
    pallas_call x1, Pallas kernels, decode(): pl.pallas_call(kernel, in_specs=[smem, smem, hbm, hbm, hbm, hbm, pl.Block...  44.7 us
    unnamed x2, local copies, waits for them, and re-layouts  6.5 us

profile of v2, /device:TPU:0, one launch (start us, length us, event | category | flops | bytes accessed | tf_op | source)
XLA Modules:
  0.0 51.2 jit_solution(17188012438837972952)
XLA Ops:
  0.0 2.2 %copy.8.wu_hbm = bf16[3,3,3,128,64]{4,3,2,1,0:T(8,128)(2,1)} copy(bf16[3,3,3,128,64]{3,4,2,1,0:T(8,128)(2,1)} %param.8) | data formatting | bytes 884736 | tf_op args[1]
  2.2 44.7 %decode.1 = bf16[32,256,128]{2,1,0:T(8,128)(2,1)} custom-call(s32[16]{0:T(128)} %ids.1, s32[16]{0:T(128)} %owner.1, bf16[4,64,64,128]{3,2,1,0:T(8,128)(2,1)} %lat_hbm.1, bf16[3,3,3,128,64]{4,3,2,1,0:T(8,128)(2,1)} %copy.8.wu_hbm, bf16[3,3,3,64,64]{4,3,2,1,0:T(8,128)(2,1)} %w1_hbm.1, bf16[3,3,3,64,64]{4,3,2,1,0:T(8,128)(2,1)} %w2_hbm.1, s32[16,27]{1,0:T(8,128)} %near_ref.1), custom_call_target="tpu_custom_call" | custom-call | tf_op jit(solution)/shard_map/decode/pallas_call | solution.py:370
  46.9 4.3 %copy.11 = bf16[4,8,256,128]{3,1,2,0:T(8,128)(2,1)} copy(bf16[4,8,256,128]{3,2,1,0:T(8,128)(2,1)} %bitcast.4) | data formatting | bytes 4194304

commit v3 on v2

--- a/solution.py
+++ b/solution.py
@@ -20,13 +20,6 @@
     key=lambda s: -(min(s[0], 4 - s[0]) + min(s[1], 4 - s[1])),
 )
 UP_TAP = ((1, 2), (None, 0))
-PHASES = (
-    ((2, 5), (2, 7), ((1, 0), (1, 1), (2, 0), (2, 1), (3, 0), (3, 1), (4, 0))),
-    ((0, 2), (0, 2), ((0, 0), (0, 1))),
-    ((5, 8), (7, 10), ((4, 1), (5, 0), (5, 1))),
-)
-
-
 def kernel(
     ids,
     owner,
@@ -52,10 +45,9 @@
     hid,
     emask,
     hmask,
-    fin,
+    pick,
     send,
     near_ids,
-    inv,
     lat_sem,
     w_sem,
     id_send,
@@ -90,17 +82,17 @@
     for c in w_copies:
         c.start()
 
-    slot = []
+    col_id = lax.broadcasted_iota(jnp.int32, (512, 256), 1)
+    row_id = lax.broadcasted_iota(jnp.int32, (512, 256), 0)
+    slot = jnp.full((1, 256), -1, jnp.int32)
+    entry = lax.broadcasted_iota(jnp.int32, (1, 256), 1) % NB
     for b in range(NB):
         rank = 0
         for r in range(b):
             rank = rank + jnp.where(owner[r] == owner[b], 1, 0)
-        slot.append(jnp.where(ids[b] >= 0, owner[b] * 2 + rank, -1))
-    for s in range(32):
-        source = -1
-        for b in range(NB):
-            source = jnp.where(slot[b] == s, b, source)
-        inv[s] = source
+        slot = jnp.where(entry == b, jnp.where(ids[b] >= 0, owner[b] * 2 + rank, -1), slot)
+    hit = (row_id // NB == slot) & (row_id % NB == col_id // NB)
+    pick[...] = jnp.where(hit, 1.0, 0.0).astype(BF16)
 
     entry = lax.broadcasted_iota(jnp.int32, (NB, 27), 0)
     n = lax.broadcasted_iota(jnp.int32, (NB, 27), 1)
@@ -128,6 +120,44 @@
                         first, emask[cx, pair[cy][py], za], emask[cx, pair[cy][py], zb]
                     )
 
+    for c in w_copies:
+        c.wait()
+
+    def wu_step(kx, _):
+        for sy in range(2):
+            for sz in range(2):
+                parts = []
+                for py in range(2):
+                    for pz in range(2):
+                        ky, kz = UP_TAP[sy][py], UP_TAP[sz][pz]
+                        parts.append(
+                            jnp.zeros((64, 128), BF16) if ky is None or kz is None else wu_raw[kx, ky, kz]
+                        )
+                at = (sy * 2 + sz) * 128
+                wu[kx, :, at : at + 128] = jnp.concatenate(parts, 0)
+        return 0
+
+    lax.fori_loop(0, 3, wu_step, 0)
+
+    def patch_weights(src, dst):
+        def step(kx, _):
+            zero = jnp.zeros((64, 64), BF16)
+
+            def pick(ky, kz):
+                return src[kx, ky, kz] if 0 <= ky < 3 and 0 <= kz < 3 else zero
+
+            for ty in range(4):
+                for tz in range(4):
+                    parts = [pick(ty - py, tz - pz) for py in range(2) for pz in range(2)]
+                    at = (ty * 4 + tz) * 64
+                    dst[kx, at : at + 64] = jnp.concatenate(parts, 1)
+            return 0
+
+        lax.fori_loop(0, 3, step, 0)
+
+    patch_weights(w1_raw, w1)
+    patch_weights(w2_raw, w2)
+
     pl.semaphore_wait(barrier, len(PEERS))
     id_up = pltpu.make_async_remote_copy(
         ids, near_ids.at[0], id_send.at[0], id_recv.at[0], device_id={"grp": me + 1}, device_id_type=MESH
@@ -199,44 +229,6 @@
         gather(3, lambda b: near_ids[1, b], to_next, 0)
         halo_up.start()
 
-    for c in w_copies:
-        c.wait()
-
-    def wu_step(kx, _):
-        for sy in range(2):
-            for sz in range(2):
-                parts = []
-                for py in range(2):
-                    for pz in range(2):
-                        ky, kz = UP_TAP[sy][py], UP_TAP[sz][pz]
-                        parts.append(
-                            jnp.zeros((128, 64), BF16) if ky is None or kz is None else wu_raw[kx, ky, kz]
-                        )
-                at = (sy * 2 + sz) * 128
-                wu[kx, at : at + 128] = jnp.concatenate(parts, 1)
-        return 0
-
-    lax.fori_loop(0, 3, wu_step, 0)
-
-    def patch_weights(src, dst):
-        def step(kx, _):
-            zero = jnp.zeros((64, 64), BF16)
-
-            def pick(ky, kz):
-                return src[kx, ky, kz] if 0 <= ky < 3 and 0 <= kz < 3 else zero
-
-            for ty in range(4):
-                for tz in range(4):
-                    parts = [pick(ty - py, tz - pz) for py in range(2) for pz in range(2)]
-                    at = (ty * 4 + tz) * 64
-                    dst[kx, at : at + 64] = jnp.concatenate(parts, 1)
-            return 0
-
-        lax.fori_loop(0, 3, step, 0)
-
-    patch_weights(w1_raw, w1)
-    patch_weights(w2_raw, w2)
-
     def spread(m, n):
         m = jnp.concatenate([m[0:1]] + [m[1:2]] * (n - 2) + [m[2:3]], 0)
         return jnp.concatenate([m[:, 0:1]] + [m[:, 1:2]] * (n - 2) + [m[:, 2:3]], 1)
@@ -244,7 +236,12 @@
     def dot(a, b):
         return jnp.dot(a, b, preferred_element_type=F32)
 
-    def up_plane(sub, parity):
+    def dot_t(a, b):
+        return lax.dot_general(a, b, (((1,), (1,)), ((), ())), preferred_element_type=F32)
+
+    def up_plane(e):
+        sub = e // 2
+
         def patch(i):
             return jnp.concatenate(
                 [
@@ -255,14 +252,19 @@
                 1,
             )
 
-        if parity:
-            value = dot(patch(sub), wu[2]) + dot(patch(sub + 1), wu[0])
-        else:
-            value = dot(patch(sub), wu[1])
-        m = spread(emask[(sub >= 1) + (sub >= 5)], 6)
-        for h in range(2):
-            part = value[:, h * 128 : h * 128 + 128].reshape(6, 6, NB, 128)
-            ext[2 * sub + parity, :, :, h] = (part * m).astype(BF16)
+        def put(value):
+            m = spread(emask[(e >= 2).astype(jnp.int32) + (e >= 10).astype(jnp.int32)], 6)
+            for h in range(2):
+                part = value[:, h * 128 : h * 128 + 128].reshape(6, 6, NB, 128)
+                ext[e, :, :, h] = (part * m).astype(BF16)
+
+        @pl.when(e % 2 == 0)
+        def _():
+            put(dot_t(patch(sub), wu[1]))
+
+        @pl.when(e % 2 == 1)
+        def _():
+            put(dot_t(patch(sub), wu[2]) + dot_t(patch(sub + 1), wu[0]))
 
     def conv(src, x, n, w_ref):
         total = None
@@ -280,75 +282,72 @@
             total = term if total is None else total + term
         return total
 
-    def first_step(x, _):
+    def first_plane(x):
         v = conv(ext, x, 5, w1)
         v = (0.5 * v) * (1.0 + jnp.tanh(0.5 * v))
         m = hmask[(x >= 1).astype(jnp.int32) + (x >= 9).astype(jnp.int32)]
         for h in range(2):
             part = v[:, h * 128 : h * 128 + 128].reshape(5, 5, NB, 128)
             hid[x, :, :, h] = (part * spread(m[:, :, h], 5)).astype(BF16)
+
+    def second_plane(x):
+        v = conv(hid, x, 4, w2)
+        own = [ext[x + 2, 1:5, 1:5, h].reshape(16 * NB, 128) for h in range(2)]
+        v = (v + jnp.concatenate(own, 1).astype(F32)).astype(BF16)
+        placed = dot(pick[...], v).astype(BF16)
+        for h in range(2):
+            send[:, x, h] = placed[:, h * 128 : h * 128 + 128].reshape(32, NB, 128)
+
+    def plane_copy(k, x):
+        dy, dx = PEERS[k]
+        to = peer(dy, dx)
+        return pltpu.make_async_remote_copy(
+            send.at[pl.ds(2 * to, 2), x],
+            out_ref.at[pl.ds(2 * me, 2), x],
+            send_sem.at[k],
+            recv_sem.at[k],
+            device_id={"grp": to},
+            device_id_type=MESH,
+        )
+
+    up_plane(jnp.int32(2))
+    up_plane(jnp.int32(3))
+
+    def step(t, _):
+        h = jnp.where(t < 5, t + 2, jnp.where(t < 7, 6 - t, t))
+        x = jnp.where(t < 5, h - 2, jnp.where(t < 7, h, h - 2))
+
+        @pl.when((t == 5) & (me == 0))
+        def _():
+            reg[0] = jnp.zeros(reg.shape[1:], BF16)
+
+        @pl.when((t == 5) & (me > 0))
+        def _():
+            halo_up.wait_recv()
+
+        @pl.when((t == 7) & (me == count - 1))
+        def _():
+            reg[5:7] = jnp.zeros((2,) + reg.shape[1:], BF16)
+
+        @pl.when((t == 7) & (me < count - 1))
+        def _():
+            halo_down.wait_recv()
+
+        up_plane(jnp.where(t < 5, h + 2, jnp.where(t < 7, h, h + 2)))
+        first_plane(h)
+
+        @pl.when(t >= 2)
+        def _():
+            second_plane(x)
+            for k in range(len(PEERS)):
+                plane_copy(k, x).start()
+
         return 0
 
-    def second_step(x, _):
-        v = conv(hid, x, 4, w2)
-        for py in range(2):
-            part = v[:, py * 128 : py * 128 + 128].reshape(4, 4, NB, 128)
-            part = part + ext[x + 2, 1:5, 1:5, py].astype(F32)
-            for cy in range(4):
-                fin[pl.ds((2 * cy + py) * 4 * NB, 4 * NB), :] = part[cy].reshape(4 * NB, 128)
-        for s in range(32):
-            b = jnp.maximum(inv[s], 0)
-            filled = inv[s] >= 0
-            for g in range(2):
-                rows = fin[pl.ds(g * 256 + b, NB, stride=NB), :]
-                at = pl.multiple_of(x * 32 + g * 16, 16)
-                send[s, pl.ds(at, 16), :] = jnp.where(filled, rows, 0.0).astype(BF16)
-        return 0
-
-    copies = []
-    for phase, ((x0, x1), (h0, h1), planes) in enumerate(PHASES):
-        if phase == 1:
-
-            @pl.when(me == 0)
-            def _():
-                reg[0] = jnp.zeros(reg.shape[1:], BF16)
-
-            @pl.when(me > 0)
-            def _():
-                halo_up.wait_recv()
-
-        if phase == 2:
-
-            @pl.when(me == count - 1)
-            def _():
-                reg[5:7] = jnp.zeros((2,) + reg.shape[1:], BF16)
-
-            @pl.when(me < count - 1)
-            def _():
-                halo_down.wait_recv()
-
-        for sub, parity in planes:
-            up_plane(sub, parity)
-        lax.fori_loop(h0, h1, first_step, 0)
-        lax.fori_loop(x0, x1, second_step, 0)
-        cells = pl.ds(x0 * 32, (x1 - x0) * 32)
-        own = pltpu.make_async_copy(
-            send.at[pl.ds(2 * me, 2), cells], out_ref.at[pl.ds(2 * me, 2), cells], own_sem.at[phase]
-        )
-        for k, (dy, dx) in enumerate(PEERS):
-            to = peer(dy, dx)
-            c = pltpu.make_async_remote_copy(
-                send.at[pl.ds(2 * to, 2), cells],
-                out_ref.at[pl.ds(2 * me, 2), cells],
-                send_sem.at[phase, k],
-                recv_sem.at[phase, k],
-                device_id={"grp": to},
-                device_id_type=MESH,
-            )
-            c.start()
-            copies.append(c)
-        own.start()
-        copies.append(own)
+    lax.fori_loop(0, 10, step, 0)
+
+    own = pltpu.make_async_copy(send.at[pl.ds(2 * me, 2)], out_ref.at[pl.ds(2 * me, 2)], own_sem.at[0])
+    own.start()
 
     @pl.when(me < count - 1)
     def _():
@@ -360,8 +359,17 @@
         id_down.wait_send()
         halo_down.wait_send()
 
-    for c in copies:
-        c.wait()
+    own.wait()
+    for k, (dy, dx) in enumerate(PEERS):
+        to = peer(dy, dx)
+        pltpu.make_async_remote_copy(
+            send.at[pl.ds(2 * to, 2)],
+            out_ref.at[pl.ds(2 * me, 2)],
+            send_sem.at[k],
+            recv_sem.at[k],
+            device_id={"grp": to},
+            device_id_type=MESH,
+        ).wait()
 
 
 def decode(ids, owner, latents, wu, w1, w2, near):
@@ -371,13 +379,13 @@
         kernel,
         in_specs=[smem, smem, hbm, hbm, hbm, hbm, pl.BlockSpec(memory_space=VMEM)],
         out_specs=hbm,
-        out_shape=jax.ShapeDtypeStruct((32, 256, 128), BF16),
+        out_shape=jax.ShapeDtypeStruct((32, 8, 2, NB, 128), BF16),
         scratch_shapes=[
             VMEM((4, G, G, 128), BF16),
-            VMEM((3, 3, 3, 128, 64), BF16),
+            VMEM((3, 3, 3, 64, 128), BF16),
             VMEM((3, 3, 3, 64, 64), BF16),
             VMEM((3, 3, 3, 64, 64), BF16),
-            VMEM((3, 512, 256), BF16),
+            VMEM((3, 256, 512), BF16),
             VMEM((3, 1024, 256), BF16),
             VMEM((3, 1024, 256), BF16),
             VMEM((4, 67, 80, 128), F32),
@@ -389,19 +397,18 @@
             VMEM((10, 5, 5, 2, NB, 128), BF16),
             VMEM((3, 3, 3, NB, 128), F32),
             VMEM((3, 3, 3, 2, NB, 128), F32),
-            VMEM((32 * NB, 128), F32),
-            VMEM((32, 256, 128), BF16),
+            VMEM((512, 256), BF16),
+            VMEM((32, 8, 2, NB, 128), BF16),
             SMEM((2, NB), jnp.int32),
-            SMEM((32,), jnp.int32),
             DMA((4,)),
             DMA((3,)),
             DMA((2,)),
             DMA((2,)),
             DMA((2,)),
             DMA((2,)),
-            DMA((3,)),
-            DMA((3, 15)),
-            DMA((3, 15)),
+            DMA((1,)),
+            DMA((15,)),
+            DMA((15,)),
         ],
         compiler_params=pltpu.CompilerParams(
             collective_id=0, has_side_effects=True, vmem_limit_bytes=56 << 20
@@ -410,9 +417,42 @@
     )(ids, owner, latents, wu, w1, w2, near)
 
 
+def order_kernel(in_ref, out_ref, turn):
+    @pl.when(pl.program_id(0) == 0)
+    def _():
+        i = lax.broadcasted_iota(jnp.int32, (256, 256), 0)
+        j = lax.broadcasted_iota(jnp.int32, (256, 256), 1)
+        hit = (i // 8 % NB == j % NB) & (i // 128 * 8 + i % 8 == j // NB)
+        turn[...] = jnp.where(hit, 1.0, 0.0).astype(BF16)
+
+    for half in range(2):
+        rows = [in_ref[half * 16 : half * 16 + 16, 0, h].reshape(256, 128) for h in range(2)]
+        v = jnp.dot(turn[...], jnp.concatenate(rows, 1), preferred_element_type=F32).astype(BF16)
+        for block in range(2):
+            for cy in range(4):
+                for h in range(2):
+                    at = block * 128 + cy * 32
+                    to = (2 * cy + h) * 32
+                    out_ref[2 * half + block, to : to + 32] = v[at : at + 32, h * 128 : h * 128 + 128]
+
+
+def ordered(rows):
+    out = pl.pallas_call(
+        order_kernel,
+        grid=(8,),
+        in_specs=[pl.BlockSpec((32, 1, 2, NB, 128), lambda i: (0, i, 0, 0, 0))],
+        out_specs=pl.BlockSpec((4, 256, 128), lambda i: (0, i, 0)),
+        out_shape=jax.ShapeDtypeStruct((4, 2048, 128), BF16),
+        scratch_shapes=[VMEM((256, 256), BF16)],
+        name="order",
+    )(rows)
+    return out.reshape(4, 256, 8, 128).transpose(0, 2, 1, 3).reshape(32, 32768)
+
+
 def local(latents, up_weight, first_weight, second_weight, brick_ids, brick_owner, neighbor_live):
-    rows = decode(brick_ids, brick_owner, latents, up_weight, first_weight, second_weight, neighbor_live)
-    return rows.reshape(32, 32768)
+    turned = jnp.swapaxes(up_weight, 3, 4)
+    rows = decode(brick_ids, brick_owner, latents, turned, first_weight, second_weight, neighbor_live)
+    return ordered(rows)
 
 
 def solution(mesh):

time: 51.9 us -> 50.4 us (0.971)
  local copies, waits for them, and re-layouts: 6.5 us -> 0 us
  Pallas kernels: 44.7 us -> 50.1 us
    pallas_call x0 -> x1, Pallas kernels: none -> 6.51 us  [ordered(): pl.pallas_call(order_kernel, grid=(8,), in_specs=[pl.BlockSpec((32, 1, 2,...]
    unnamed x2 -> x0, local copies, waits for them, and re-layouts: 6.5 us -> none
    pallas_call x1, Pallas kernels: 44.7 us -> 43.6 us  [decode(): pl.pallas_call(kernel, in_specs=[smem, smem, hbm, hbm, hbm, hbm, pl.Block...]
where the time goes in v3:
time: 50.4 us; the launch traced here: 50.1 us
  Pallas kernels  50.1 us (99%)
    pallas_call x1, Pallas kernels, decode(): pl.pallas_call(kernel, in_specs=[smem, smem, hbm, hbm, hbm, hbm, pl.Block...  43.6 us
    pallas_call x1, Pallas kernels, ordered(): pl.pallas_call(order_kernel, grid=(8,), in_specs=[pl.BlockSpec((32, 1, 2,...  6.51 us

profile of v3, /device:TPU:0, one launch (start us, length us, event | category | flops | bytes accessed | tf_op | source)
XLA Modules:
  0.0 50.1 jit_solution(1963863061521118799)
XLA Ops:
  0.0 43.6 %decode.1.in_ref = bf16[32,8,2,16,128]{4,3,2,1,0:T(8,128)(2,1)} custom-call(s32[16]{0:T(128)} %ids.1, s32[16]{0:T(128)} %owner.1, bf16[4,64,64,128]{3,2,1,0:T(8,128)(2,1)} %lat_hbm.1, bf16[3,3,3,64,128]{4,3,2,1,0:T(8,128)(2,1)} %bitcast.6, bf16[3,3,3,64,64]{4,3,2,1,0:T(8,128)(2,1)} %w1_hbm.1, bf16[3,3,3,64,64]{4,3,2,1,0:T(8,128)(2,1)} %w2_hbm.1, ...), custom_call_target="tpu_custom_call" | custom-call | tf_op jit(solution)/shard_map/decode/pallas_call | solution.py:378
  43.6 6.5 %order.1 = bf16[4,2048,128]{2,1,0:T(8,128)(2,1)} custom-call(bf16[32,8,2,16,128]{4,3,2,1,0:T(8,128)(2,1)} %decode.1.in_ref), custom_call_target="tpu_custom_call" | custom-call | tf_op jit(solution)/shard_map/order/pallas_call | solution.py:440

commit v4 on v2

v4 whole, which is shorter than its diff:
```python
import jax
import jax.numpy as jnp
from jax import lax
from jax.experimental import pallas as pl
from jax.experimental.pallas import tpu as pltpu
from jax.sharding import PartitionSpec as P

G = 64
HB = 4
NB = 16
VMEM = pltpu.VMEM
SMEM = pltpu.SMEM
DMA = pltpu.SemaphoreType.DMA
F32 = jnp.float32
BF16 = jnp.bfloat16
MESH = pl.DeviceIdType.MESH

PEERS = sorted(
    ((dy, dx) for dy in range(4) for dx in range(4) if dy or dx),
    key=lambda s: -(min(s[0], 4 - s[0]) + min(s[1], 4 - s[1])),
)
UP_TAP = ((1, 2), (None, 0))
EXT_ORDER = (2, 3, 4, 5, 6, 7, 8, 1, 0, 9, 10, 11)
HID_ORDER = (2, 3, 4, 5, 6, 1, 0, 7, 8, 9)
OUT_ORDER = (2, 3, 4, 1, 0, 5, 6, 7)


def kernel(
    ids,
    owner,
    lat_hbm,
    wu_hbm,
    w1_hbm,
    w2_hbm,
    near_ref,
    out_ref,
    lat,
    wu_raw,
    w1_raw,
    w2_raw,
    wu,
    w1,
    w2,
    pan,
    win,
    reg,
    to_prev,
    to_next,
    ext,
    hid,
    emask,
    hmask,
    pick,
    turn,
    done,
    send,
    recv,
    stage,
    near_ids,
    lat_sem,
    w_sem,
    id_send,
    id_recv,
    halo_send,
    halo_recv,
    own_sem,
    out_sem,
    send_sem,
    recv_sem,
):
    count = lax.axis_size("grp")
    me = lax.axis_index("grp")
    row, col = me // 4, me % 4
    after, before = (me + 1) % count, (me + count - 1) % count
    across = G // HB

    def peer(dy, dx):
        return (row + dy) % 4 * 4 + (col + dx) % 4

    barrier = pltpu.get_barrier_semaphore()
    for dy, dx in PEERS:
        pl.semaphore_signal(barrier, inc=1, device_id={"grp": peer(dy, dx)}, device_id_type=MESH)

    def lat_copy(p):
        return pltpu.make_async_copy(lat_hbm.at[p], lat.at[p], lat_sem.at[p])

    w_copies = [
        pltpu.make_async_copy(s, d, w_sem.at[i])
        for i, (s, d) in enumerate(((wu_hbm, wu_raw), (w1_hbm, w1_raw), (w2_hbm, w2_raw)))
    ]
    for p in (0, 1, 3):
        lat_copy(p).start()
    w_copies[0].start()
    w_copies[1].start()
    lat_copy(2).start()
    w_copies[2].start()

    def border(p, _):
        pan[p, 0] = jnp.zeros(pan.shape[2:], F32)
        pan[p, 65:67] = jnp.zeros((2,) + pan.shape[2:], F32)
        pan[p, :, 0:8] = jnp.zeros((67, 8, 128), F32)
        pan[p, :, 72:80] = jnp.zeros((67, 8, 128), F32)
        return 0

    lax.fori_loop(0, 4, border, 0)

    def load_plane(p):
        lat_copy(p).wait()
        pan[p, 1:65, 8:72] = lat[p].astype(F32)

    def gather(p, id_of, dst, q):
        def one(b, _):
            local = jnp.maximum(id_of(b), 0)
            by = local // across % across
            bz = local % across
            for j in range(7):
                win[pl.ds(pl.multiple_of((j * NB + b) * 8, 8), 8), :] = pan[p, 4 * by + j, pl.ds(4 * bz + 7, 8), :]
            return 0

        lax.fori_loop(0, NB, one, 0)

        def two(j, _):
            for l in range(7):
                dst[q, j, l] = win[pl.ds(j * 128 + l, NB, stride=8), :].astype(BF16)
            return 0

        lax.fori_loop(0, 7, two, 0)

    pl.semaphore_wait(barrier, len(PEERS))
    id_up = pltpu.make_async_remote_copy(
        ids, near_ids.at[0], id_send.at[0], id_recv.at[0], device_id={"grp": after}, device_id_type=MESH
    )
    id_down = pltpu.make_async_remote_copy(
        ids, near_ids.at[1], id_send.at[1], id_recv.at[1], device_id={"grp": before}, device_id_type=MESH
    )
    id_up.start()
    id_down.start()

    halo_up = pltpu.make_async_remote_copy(
        to_next, reg.at[pl.ds(0, 1)], halo_send.at[0], halo_recv.at[0], device_id={"grp": after}, device_id_type=MESH
    )
    halo_down = [
        pltpu.make_async_remote_copy(
            to_prev.at[i],
            reg.at[5 + i],
            halo_send.at[1 + i],
            halo_recv.at[1 + i],
            device_id={"grp": before},
            device_id_type=MESH,
        )
        for i in range(2)
    ]
    load_plane(0)
    gather(0, lambda b: ids[b], reg, 1)
    load_plane(1)
    id_up.wait()
    for p in range(2):
        gather(p, lambda b: near_ids[0, b], to_prev, p)
        halo_down[p].start()
    load_plane(3)
    id_down.wait()
    gather(3, lambda b: near_ids[1, b], to_next, 0)
    halo_up.start()
    gather(1, lambda b: ids[b], reg, 2)
    load_plane(2)
    gather(2, lambda b: ids[b], reg, 3)

    entry = lax.broadcasted_iota(jnp.int32, (NB, 27), 0)
    n = lax.broadcasted_iota(jnp.int32, (NB, 27), 1)
    local = jnp.full((NB, 27), -1, jnp.int32)
    for b in range(NB):
        local = jnp.where(entry == b, ids[b], local)
    used = local >= 0
    local = jnp.maximum(local, 0)
    near_x = me + local // (across * across) + n // 9 - 1
    near_y = local // across % across + n // 3 % 3 - 1
    near_z = local % across + n % 3 - 1
    inside = (near_x >= 0) & (near_x < count) & (near_y >= 0) & (near_y < across)
    inside = inside & (near_z >= 0) & (near_z < across)
    live = jnp.where(inside & ((near_ref[...] > 0) | (n == 13)) & used, 1.0, 0.0)
    for k in range(27):
        emask[k // 9, k // 3 % 3, k % 3] = jnp.broadcast_to(live[:, k : k + 1], (NB, 128))
    first = lax.broadcasted_iota(jnp.int32, (NB, 128), 1) < 64
    pair = ((0, 1), (1, 1), (1, 2))
    for cx in range(3):
        for cy in range(3):
            for cz in range(3):
                for py in range(2):
                    za, zb = pair[cz]
                    hmask[cx, cy, cz, py] = jnp.where(
                        first, emask[cx, pair[cy][py], za], emask[cx, pair[cy][py], zb]
                    )

    w_copies[0].wait()

    def wu_step(kx, _):
        for sy in range(2):
            for sz in range(2):
                parts = []
                for py in range(2):
                    for pz in range(2):
                        ky, kz = UP_TAP[sy][py], UP_TAP[sz][pz]
                        parts.append(
                            jnp.zeros((64, 128), BF16) if ky is None or kz is None else wu_raw[kx, ky, kz]
                        )
                at = (sy * 2 + sz) * 128
                wu[kx, at : at + 128] = jnp.concatenate(parts, 0).T
        return 0

    lax.fori_loop(0, 3, wu_step, 0)

    def patch_weights(src, dst):
        def step(kx, _):
            zero = jnp.zeros((64, 64), BF16)

            def pick(ky, kz):
                return src[kx, ky, kz] if 0 <= ky < 3 and 0 <= kz < 3 else zero

            for ty in range(4):
                for tz in range(4):
                    parts = [pick(ty - py, tz - pz) for py in range(2) for pz in range(2)]
                    at = (ty * 4 + tz) * 64
                    dst[kx, at : at + 64] = jnp.concatenate(parts, 1)
            return 0

        lax.fori_loop(0, 3, step, 0)

    w_copies[1].wait()
    patch_weights(w1_raw, w1)
    w_copies[2].wait()
    patch_weights(w2_raw, w2)

    col_id = lax.broadcasted_iota(jnp.int32, (512, 256), 1)
    row_id = lax.broadcasted_iota(jnp.int32, (512, 256), 0)
    slot = jnp.full((1, 256), -1, jnp.int32)
    entry = lax.broadcasted_iota(jnp.int32, (1, 256), 1) % NB
    for b in range(NB):
        rank = 0
        for r in range(b):
            rank = rank + jnp.where(owner[r] == owner[b], 1, 0)
        slot = jnp.where(entry == b, jnp.where(ids[b] >= 0, owner[b] * 2 + rank, -1), slot)
    hit = (row_id // NB == slot) & (row_id % NB == col_id // NB)
    pick[...] = jnp.where(hit, 1.0, 0.0).astype(BF16)

    def spread(m, n):
        m = jnp.concatenate([m[0:1]] + [m[1:2]] * (n - 2) + [m[2:3]], 0)
        return jnp.concatenate([m[:, 0:1]] + [m[:, 1:2]] * (n - 2) + [m[:, 2:3]], 1)

    def dot(a, b):
        return jnp.dot(a, b, preferred_element_type=F32)

    def up_plane(e):
        sub = e // 2

        def patch(i):
            return jnp.concatenate(
                [
                    reg[i, sy : sy + 6, sz : sz + 6].reshape(36 * NB, 128)
                    for sy in range(2)
                    for sz in range(2)
                ],
                1,
            )

        if e % 2:
            value = dot(patch(sub), wu[2]) + dot(patch(sub + 1), wu[0])
        else:
            value = dot(patch(sub), wu[1])
        m = spread(emask[(e >= 2) + (e >= 10)], 6)
        for h in range(2):
            part = value[:, h * 128 : h * 128 + 128].reshape(6, 6, NB, 128)
            ext[e, :, :, h] = (part * m).astype(BF16)

    def conv(src, x, n, w_ref):
        total = None
        for kx in range(3):
            patch = jnp.concatenate(
                [
                    src[x + kx, dy : dy + n, dz : dz + n, qy].reshape(n * n * NB, 128)
                    for dy in range(2)
                    for qy in range(2)
                    for dz in range(2)
                ],
                1,
            )
            term = dot(patch, w_ref[kx])
            total = term if total is None else total + term
        return total

    def first_plane(x):
        v = conv(ext, x, 5, w1)
        v = (0.5 * v) * (1.0 + jnp.tanh(0.5 * v))
        m = hmask[(x >= 1) + (x >= 9)]
        for h in range(2):
            part = v[:, h * 128 : h * 128 + 128].reshape(5, 5, NB, 128)
            hid[x, :, :, h] = (part * spread(m[:, :, h], 5)).astype(BF16)

    def second_plane(x):
        v = conv(hid, x, 4, w2)
        own = [ext[x + 2, 1:5, 1:5, h].reshape(16 * NB, 128) for h in range(2)]
        done[x] = (v + jnp.concatenate(own, 1).astype(F32)).astype(BF16)

    def plane_copy(k, x):
        dy, dx = PEERS[k]
        to = peer(dy, dx)
        return pltpu.make_async_remote_copy(
            send.at[x, pl.ds(2 * to, 2)],
            recv.at[x, pl.ds(2 * me, 2)],
            send_sem.at[x, k],
            recv_sem.at[x, k],
            device_id={"grp": to},
            device_id_type=MESH,
        )

    def own_copy(x):
        return pltpu.make_async_copy(send.at[x, pl.ds(2 * me, 2)], recv.at[x, pl.ds(2 * me, 2)], own_sem.at[x])

    def send_plane(x):
        placed = dot(pick[...], done[x]).astype(BF16)
        for h in range(2):
            send[x, :, h] = placed[:, h * 128 : h * 128 + 128].reshape(32, NB, 128)
        for k in range(len(PEERS)):
            plane_copy(k, x).start()
        own_copy(x).start()

    for e in EXT_ORDER[:3]:
        up_plane(e)

    for t in range(10):
        first_plane(HID_ORDER[t])
        if t >= 2:
            second_plane(OUT_ORDER[t - 2])
            send_plane(OUT_ORDER[t - 2])
        if t + 3 < 12:
            e = EXT_ORDER[t + 3]
            if e == 7:
                gather(3, lambda b: ids[b], reg, 4)
            if e == 1:
                halo_up.wait_recv()
            if e == 9:
                for c in halo_down:
                    c.wait_recv()

                @pl.when(me == count - 1)
                def _():
                    reg[5:7] = jnp.zeros((2,) + reg.shape[1:], BF16)

            up_plane(e)

    i = lax.broadcasted_iota(jnp.int32, (256, 256), 0)
    j = lax.broadcasted_iota(jnp.int32, (256, 256), 1)
    hit = (i // 8 % NB == j % NB) & (i // 128 * 8 + i % 8 == j // NB)
    turn[...] = jnp.where(hit, 1.0, 0.0).astype(BF16)

    def out_copy(x):
        cells = pl.ds(x * 256, 256)
        return pltpu.make_async_copy(stage.at[:, cells], out_ref.at[:, cells], out_sem.at[x])

    def arrive(n, _):
        x = jnp.where(n < 3, n + 2, jnp.where(n < 5, 4 - n, n))
        own_copy(x).wait()
        for k in range(len(PEERS)):
            plane_copy(k, x).wait()
        for half in range(2):
            rows = [recv[x, half * 16 : half * 16 + 16, h].reshape(256, 128) for h in range(2)]
            v = dot(turn[...], jnp.concatenate(rows, 1)).astype(BF16)
            for block in range(2):
                for cy in range(4):
                    for h in range(2):
                        at = block * 128 + cy * 32
                        to = pl.multiple_of(x * 256 + (2 * cy + h) * 32, 32)
                        stage[2 * half + block, pl.ds(to, 32)] = v[at : at + 32, h * 128 : h * 128 + 128]
        out_copy(x).start()
        return 0

    lax.fori_loop(0, 8, arrive, 0)
    halo_up.wait_send()
    for c in halo_down:
        c.wait_send()
    for x in range(8):
        out_copy(x).wait()


def decode(ids, owner, latents, wu, w1, w2, near):
    smem = pl.BlockSpec(memory_space=SMEM)
    hbm = pl.BlockSpec(memory_space=pl.ANY)
    return pl.pallas_call(
        kernel,
        in_specs=[smem, smem, hbm, hbm, hbm, hbm, pl.BlockSpec(memory_space=VMEM)],
        out_specs=hbm,
        out_shape=jax.ShapeDtypeStruct((4, 2048, 128), BF16),
        scratch_shapes=[
            VMEM((4, G, G, 128), BF16),
            VMEM((3, 3, 3, 64, 128), BF16),
            VMEM((3, 3, 3, 64, 64), BF16),
            VMEM((3, 3, 3, 64, 64), BF16),
            VMEM((3, 512, 256), BF16),
            VMEM((3, 1024, 256), BF16),
            VMEM((3, 1024, 256), BF16),
            VMEM((4, 67, 80, 128), F32),
            VMEM((7 * NB * 8, 128), F32),
            VMEM((7, 7, 7, NB, 128), BF16),
            VMEM((2, 7, 7, NB, 128), BF16),
            VMEM((1, 7, 7, NB, 128), BF16),
            VMEM((12, 6, 6, 2, NB, 128), BF16),
            VMEM((10, 5, 5, 2, NB, 128), BF16),
            VMEM((3, 3, 3, NB, 128), F32),
            VMEM((3, 3, 3, 2, NB, 128), F32),
            VMEM((512, 256), BF16),
            VMEM((256, 256), BF16),
            VMEM((8, 256, 256), BF16),
            VMEM((8, 32, 2, NB, 128), BF16),
            VMEM((8, 32, 2, NB, 128), BF16),
            VMEM((4, 2048, 128), BF16),
            SMEM((2, NB), jnp.int32),
            DMA((4,)),
            DMA((3,)),
            DMA((2,)),
            DMA((2,)),
            DMA((3,)),
            DMA((3,)),
            DMA((8,)),
            DMA((8,)),
            DMA((8, 15)),
            DMA((8, 15)),
        ],
        compiler_params=pltpu.CompilerParams(
            collective_id=0, has_side_effects=True, vmem_limit_bytes=56 << 20
        ),
        name="decode",
    )(ids, owner, latents, wu, w1, w2, near)


def hand_over(rows):
    def body(in_ref, out_ref, held, in_sem, out_sem):
        parts = [(i // 2, pl.ds(i % 2 * 1024, 1024)) for i in range(8)]
        loads = [pltpu.make_async_copy(in_ref.at[p], held.at[p], in_sem.at[i]) for i, p in enumerate(parts)]
        stores = [pltpu.make_async_copy(held.at[p], out_ref.at[p], out_sem.at[i]) for i, p in enumerate(parts)]
        for c in loads:
            c.start()
        for c, d in zip(loads, stores):
            c.wait()
            d.start()
        for d in stores:
            d.wait()

    hbm = pl.BlockSpec(memory_space=pl.ANY)
    return pl.pallas_call(
        body,
        in_specs=[hbm],
        out_specs=hbm,
        out_shape=jax.ShapeDtypeStruct(rows.shape, rows.dtype),
        scratch_shapes=[VMEM(rows.shape, rows.dtype), DMA((8,)), DMA((8,))],
        name="hand_over",
    )(rows)


def local(latents, up_weight, first_weight, second_weight, brick_ids, brick_owner, neighbor_live):
    turned = jnp.swapaxes(up_weight, 3, 4)
    rows = decode(brick_ids, brick_owner, latents, turned, first_weight, second_weight, neighbor_live)
    rows = hand_over(rows)
    return rows.reshape(4, 256, 8, 128).transpose(0, 2, 1, 3).reshape(32, 32768)


def solution(mesh):
    rows = P(("shape", "grp"))
    in_specs = (rows, P(), P(), P(), rows, rows, rows)
    return jax.shard_map(local, mesh=mesh, in_specs=in_specs, out_specs=rows, check_vma=False)
```

time: 51.9 us -> 47.9 us (0.923); the launches traced: 51.2 us -> 47.7 us
  local copies, waits for them, and re-layouts: 6.5 us -> 0 us
  Pallas kernels: 44.7 us -> 47.6 us
    unnamed x2 -> x0, local copies, waits for them, and re-layouts: 6.5 us -> none
    pallas_call x0 -> x1, Pallas kernels: none -> 2.39 us  [hand_over(): pl.pallas_call(body, in_specs=[hbm], out_specs=hbm, out_shape=jax.ShapeDt...]
where the time goes in v4:
time: 47.9 us; the launch traced here: 47.7 us
  Pallas kernels  47.6 us (99%)
    pallas_call x1, Pallas kernels, decode(): pl.pallas_call(kernel, in_specs=[smem, smem, hbm, hbm, hbm, hbm, pl.Block...  45.2 us
    pallas_call x1, Pallas kernels, hand_over(): pl.pallas_call(body, in_specs=[hbm], out_specs=hbm, out_shape=jax.ShapeDt...  2.39 us

profile of v4, /device:TPU:0, one launch (start us, length us, event | category | flops | bytes accessed | tf_op | source)
XLA Modules:
  0.0 47.7 jit_solution(4591198975163900419)
XLA Ops:
  0.0 45.2 %decode.1.in_ref = bf16[4,2048,128]{2,1,0:T(8,128)(2,1)} custom-call(s32[16]{0:T(128)} %ids.1, s32[16]{0:T(128)} %owner.1, bf16[4,64,64,128]{3,2,1,0:T(8,128)(2,1)} %lat_hbm.1, bf16[3,3,3,64,128]{4,3,2,1,0:T(8,128)(2,1)} %bitcast.6, bf16[3,3,3,64,64]{4,3,2,1,0:T(8,128)(2,1)} %w1_hbm.1, bf16[3,3,3,64,64]{4,3,2,1,0:T(8,128)(2,1)} %w2_hbm.1, s32[16,27]{1,0:T(8,128)} %near_ref.1), custom_call_target="tpu_custom_call" | custom-call | tf_op jit(solution)/shard_map/decode/pallas_call | solution.py:387
  45.2 2.4 %hand_over.1 = bf16[4,2048,128]{2,1,0:T(8,128)(2,1)} custom-call(bf16[4,2048,128]{2,1,0:T(8,128)(2,1)} %decode.1.in_ref), custom_call_target="tpu_custom_call" | custom-call | tf_op jit(solution)/shard_map/hand_over/pallas_call | solution.py:448

commit v5 on v4

--- a/solution.py
+++ b/solution.py
@@ -109,22 +109,15 @@
         pan[p, 1:65, 8:72] = lat[p].astype(F32)
 
     def gather(p, id_of, dst, q):
-        def one(b, _):
+        for b in range(NB):
             local = jnp.maximum(id_of(b), 0)
             by = local // across % across
             bz = local % across
             for j in range(7):
-                win[pl.ds(pl.multiple_of((j * NB + b) * 8, 8), 8), :] = pan[p, 4 * by + j, pl.ds(4 * bz + 7, 8), :]
-            return 0
-
-        lax.fori_loop(0, NB, one, 0)
-
-        def two(j, _):
+                win[(j * NB + b) * 8 : (j * NB + b) * 8 + 8, :] = pan[p, 4 * by + j, pl.ds(4 * bz + 7, 8), :]
+        for j in range(7):
             for l in range(7):
                 dst[q, j, l] = win[pl.ds(j * 128 + l, NB, stride=8), :].astype(BF16)
-            return 0
-
-        lax.fori_loop(0, 7, two, 0)
 
     pl.semaphore_wait(barrier, len(PEERS))
     id_up = pltpu.make_async_remote_copy(
@@ -180,17 +173,6 @@
     live = jnp.where(inside & ((near_ref[...] > 0) | (n == 13)) & used, 1.0, 0.0)
     for k in range(27):
         emask[k // 9, k // 3 % 3, k % 3] = jnp.broadcast_to(live[:, k : k + 1], (NB, 128))
-    first = lax.broadcasted_iota(jnp.int32, (NB, 128), 1) < 64
-    pair = ((0, 1), (1, 1), (1, 2))
-    for cx in range(3):
-        for cy in range(3):
-            for cz in range(3):
-                for py in range(2):
-                    za, zb = pair[cz]
-                    hmask[cx, cy, cz, py] = jnp.where(
-                        first, emask[cx, pair[cy][py], za], emask[cx, pair[cy][py], zb]
-                    )
-
     w_copies[0].wait()
 
     def wu_step(kx, _):
@@ -210,37 +192,33 @@
     lax.fori_loop(0, 3, wu_step, 0)
 
     def patch_weights(src, dst):
-        def step(kx, _):
-            zero = jnp.zeros((64, 64), BF16)
-
-            def pick(ky, kz):
-                return src[kx, ky, kz] if 0 <= ky < 3 and 0 <= kz < 3 else zero
-
+        zero = jnp.zeros((64, 64), BF16)
+
+        def tap(kx, ky, kz):
+            return src[kx, ky, kz] if 0 <= ky < 3 and 0 <= kz < 3 else zero
+
+        for kx in range(3):
             for ty in range(4):
                 for tz in range(4):
-                    parts = [pick(ty - py, tz - pz) for py in range(2) for pz in range(2)]
+                    parts = [tap(kx, ty - py, tz - pz) for py in range(2) for pz in range(2)]
                     at = (ty * 4 + tz) * 64
                     dst[kx, at : at + 64] = jnp.concatenate(parts, 1)
-            return 0
-
-        lax.fori_loop(0, 3, step, 0)
 
     w_copies[1].wait()
     patch_weights(w1_raw, w1)
-    w_copies[2].wait()
-    patch_weights(w2_raw, w2)
-
-    col_id = lax.broadcasted_iota(jnp.int32, (512, 256), 1)
-    row_id = lax.broadcasted_iota(jnp.int32, (512, 256), 0)
-    slot = jnp.full((1, 256), -1, jnp.int32)
-    entry = lax.broadcasted_iota(jnp.int32, (1, 256), 1) % NB
-    for b in range(NB):
-        rank = 0
-        for r in range(b):
-            rank = rank + jnp.where(owner[r] == owner[b], 1, 0)
-        slot = jnp.where(entry == b, jnp.where(ids[b] >= 0, owner[b] * 2 + rank, -1), slot)
-    hit = (row_id // NB == slot) & (row_id % NB == col_id // NB)
-    pick[...] = jnp.where(hit, 1.0, 0.0).astype(BF16)
+
+    def make_pick():
+        col_id = lax.broadcasted_iota(jnp.int32, (512, 256), 1)
+        row_id = lax.broadcasted_iota(jnp.int32, (512, 256), 0)
+        slot = jnp.full((1, 256), -1, jnp.int32)
+        entry = lax.broadcasted_iota(jnp.int32, (1, 256), 1) % NB
+        for b in range(NB):
+            rank = 0
+            for r in range(b):
+                rank = rank + jnp.where(owner[r] == owner[b], 1, 0)
+            slot = jnp.where(entry == b, jnp.where(ids[b] >= 0, owner[b] * 2 + rank, -1), slot)
+        hit = (row_id // NB == slot) & (row_id % NB == col_id // NB)
+        pick[...] = jnp.where(hit, 1.0, 0.0).astype(BF16)
 
     def spread(m, n):
         m = jnp.concatenate([m[0:1]] + [m[1:2]] * (n - 2) + [m[2:3]], 0)
@@ -326,8 +304,24 @@
     for e in EXT_ORDER[:3]:
         up_plane(e)
 
+    first = lax.broadcasted_iota(jnp.int32, (NB, 128), 1) < 64
+    pair = ((0, 1), (1, 1), (1, 2))
+    for cx in range(3):
+        for cy in range(3):
+            for cz in range(3):
+                for py in range(2):
+                    za, zb = pair[cz]
+                    hmask[cx, cy, cz, py] = jnp.where(
+                        first, emask[cx, pair[cy][py], za], emask[cx, pair[cy][py], zb]
+                    )
+
     for t in range(10):
         first_plane(HID_ORDER[t])
+        if t == 0:
+            w_copies[2].wait()
+            patch_weights(w2_raw, w2)
+        if t == 1:
+            make_pick()
         if t >= 2:
             second_plane(OUT_ORDER[t - 2])
             send_plane(OUT_ORDER[t - 2])

time: 47.9 us -> 47.2 us (0.985)
  Pallas kernels: 47.6 us -> 46.6 us
    pallas_call x1, Pallas kernels: 45.2 us -> 44.2 us  [decode(): pl.pallas_call(kernel, in_specs=[smem, smem, hbm, hbm, hbm, hbm, pl.Block...]
where the time goes in v5:
time: 47.2 us; the launch traced here: 46.8 us
  Pallas kernels  46.6 us (99%)
    pallas_call x1, Pallas kernels, decode(): pl.pallas_call(kernel, in_specs=[smem, smem, hbm, hbm, hbm, hbm, pl.Block...  44.2 us
    pallas_call x1, Pallas kernels, hand_over(): pl.pallas_call(body, in_specs=[hbm], out_specs=hbm, out_shape=jax.ShapeDt...  2.39 us

profile of v5, /device:TPU:0, one launch (start us, length us, event | category | flops | bytes accessed | tf_op | source)
XLA Modules:
  0.0 46.8 jit_solution(6386718347117725363)
XLA Ops:
  0.0 44.2 %decode.1.in_ref = bf16[4,2048,128]{2,1,0:T(8,128)(2,1)} custom-call(s32[16]{0:T(128)} %ids.1, s32[16]{0:T(128)} %owner.1, bf16[4,64,64,128]{3,2,1,0:T(8,128)(2,1)} %lat_hbm.1, bf16[3,3,3,64,128]{4,3,2,1,0:T(8,128)(2,1)} %bitcast.6, bf16[3,3,3,64,64]{4,3,2,1,0:T(8,128)(2,1)} %w1_hbm.1, bf16[3,3,3,64,64]{4,3,2,1,0:T(8,128)(2,1)} %w2_hbm.1, s32[16,27]{1,0:T(8,128)} %near_ref.1), custom_call_target="tpu_custom_call" | custom-call | tf_op jit(solution)/shard_map/decode/pallas_call | solution.py:381
  44.2 2.4 %hand_over.1 = bf16[4,2048,128]{2,1,0:T(8,128)(2,1)} custom-call(bf16[4,2048,128]{2,1,0:T(8,128)(2,1)} %decode.1.in_ref), custom_call_target="tpu_custom_call" | custom-call | tf_op jit(solution)/shard_map/hand_over/pallas_call | solution.py:442

commit v6 on v5

--- a/solution.py
+++ b/solution.py
@@ -55,7 +55,6 @@
     done,
     send,
     recv,
-    stage,
     near_ids,
     lat_sem,
     w_sem,
@@ -64,7 +63,6 @@
     halo_send,
     halo_recv,
     own_sem,
-    out_sem,
     send_sem,
     recv_sem,
 ):
@@ -346,10 +344,6 @@
     hit = (i // 8 % NB == j % NB) & (i // 128 * 8 + i % 8 == j // NB)
     turn[...] = jnp.where(hit, 1.0, 0.0).astype(BF16)
 
-    def out_copy(x):
-        cells = pl.ds(x * 256, 256)
-        return pltpu.make_async_copy(stage.at[:, cells], out_ref.at[:, cells], out_sem.at[x])
-
     def arrive(n, _):
         x = jnp.where(n < 3, n + 2, jnp.where(n < 5, 4 - n, n))
         own_copy(x).wait()
@@ -363,16 +357,13 @@
                     for h in range(2):
                         at = block * 128 + cy * 32
                         to = pl.multiple_of(x * 256 + (2 * cy + h) * 32, 32)
-                        stage[2 * half + block, pl.ds(to, 32)] = v[at : at + 32, h * 128 : h * 128 + 128]
-        out_copy(x).start()
+                        out_ref[2 * half + block, pl.ds(to, 32)] = v[at : at + 32, h * 128 : h * 128 + 128]
         return 0
 
     lax.fori_loop(0, 8, arrive, 0)
     halo_up.wait_send()
     for c in halo_down:
         c.wait_send()
-    for x in range(8):
-        out_copy(x).wait()
 
 
 def decode(ids, owner, latents, wu, w1, w2, near):
@@ -381,8 +372,8 @@
     return pl.pallas_call(
         kernel,
         in_specs=[smem, smem, hbm, hbm, hbm, hbm, pl.BlockSpec(memory_space=VMEM)],
-        out_specs=hbm,
-        out_shape=jax.ShapeDtypeStruct((4, 2048, 128), BF16),
+        out_specs=pl.BlockSpec(memory_space=VMEM),
+        out_shape=VMEM((4, 2048, 128), BF16),
         scratch_shapes=[
             VMEM((4, G, G, 128), BF16),
             VMEM((3, 3, 3, 64, 128), BF16),
@@ -405,7 +396,6 @@
             VMEM((8, 256, 256), BF16),
             VMEM((8, 32, 2, NB, 128), BF16),
             VMEM((8, 32, 2, NB, 128), BF16),
-            VMEM((4, 2048, 128), BF16),
             SMEM((2, NB), jnp.int32),
             DMA((4,)),
             DMA((3,)),
@@ -413,7 +403,6 @@
             DMA((2,)),
             DMA((3,)),
             DMA((3,)),
-            DMA((8,)),
             DMA((8,)),
             DMA((8, 15)),
             DMA((8, 15)),
@@ -425,34 +414,9 @@
     )(ids, owner, latents, wu, w1, w2, near)
 
 
-def hand_over(rows):
-    def body(in_ref, out_ref, held, in_sem, out_sem):
-        parts = [(i // 2, pl.ds(i % 2 * 1024, 1024)) for i in range(8)]
-        loads = [pltpu.make_async_copy(in_ref.at[p], held.at[p], in_sem.at[i]) for i, p in enumerate(parts)]
-        stores = [pltpu.make_async_copy(held.at[p], out_ref.at[p], out_sem.at[i]) for i, p in enumerate(parts)]
-        for c in loads:
-            c.start()
-        for c, d in zip(loads, stores):
-            c.wait()
-            d.start()
-        for d in stores:
-            d.wait()
-
-    hbm = pl.BlockSpec(memory_space=pl.ANY)
-    return pl.pallas_call(
-        body,
-        in_specs=[hbm],
-        out_specs=hbm,
-        out_shape=jax.ShapeDtypeStruct(rows.shape, rows.dtype),
-        scratch_shapes=[VMEM(rows.shape, rows.dtype), DMA((8,)), DMA((8,))],
-        name="hand_over",
-    )(rows)
-
-
 def local(latents, up_weight, first_weight, second_weight, brick_ids, brick_owner, neighbor_live):
     turned = jnp.swapaxes(up_weight, 3, 4)
     rows = decode(brick_ids, brick_owner, latents, turned, first_weight, second_weight, neighbor_live)
-    rows = hand_over(rows)
     return rows.reshape(4, 256, 8, 128).transpose(0, 2, 1, 3).reshape(32, 32768)
 
 

time: 47.2 us -> 45.1 us (0.956)
  Pallas kernels: 46.6 us -> 43.4 us
  local copies, waits for them, and re-layouts: 0 us -> 1.32 us
    pallas_call x1 -> x0, Pallas kernels: 2.39 us -> none  [hand_over(): pl.pallas_call(body, in_specs=[hbm], out_specs=hbm, out_shape=jax.ShapeDt...]
    unnamed x0 -> x1, local copies, waits for them, and re-layouts: none -> 1.32 us
    pallas_call x1, Pallas kernels: 44.2 us -> 43.4 us  [decode(): pl.pallas_call(kernel, in_specs=[smem, smem, hbm, hbm, hbm, hbm, pl.Block...]
where the time goes in v6:
time: 45.1 us; the launch traced here: 44.8 us
  Pallas kernels  43.4 us (96%)
  local copies, waits for them, and re-layouts  1.32 us (3%)
    pallas_call x1, Pallas kernels, decode(): pl.pallas_call(kernel, in_specs=[smem, smem, hbm, hbm, hbm, hbm, pl.Block...  43.4 us
    unnamed x1, local copies, waits for them, and re-layouts  1.32 us

profile of v6, /device:TPU:0, one launch (start us, length us, event | category | flops | bytes accessed | tf_op | source)
XLA Modules:
  0.0 44.8 jit_solution(11831173010128771062)
XLA Ops:
  0.0 43.4 %decode.1 = bf16[4,2048,128]{2,1,0:T(8,128)(2,1)S(1)} custom-call(s32[16]{0:T(128)} %ids.1, s32[16]{0:T(128)} %owner.1, bf16[4,64,64,128]{3,2,1,0:T(8,128)(2,1)} %lat_hbm.1, bf16[3,3,3,64,128]{4,3,2,1,0:T(8,128)(2,1)} %bitcast.7, bf16[3,3,3,64,64]{4,3,2,1,0:T(8,128)(2,1)} %w1_hbm.1, bf16[3,3,3,64,64]{4,3,2,1,0:T(8,128)(2,1)} %w2_hbm.1, s32[16,27]{1,0:T(8,128)} %near_ref.1), custom_call_target="tpu_custom_call" | custom-call | tf_op jit(solution)/shard_map/decode/pallas_call | solution.py:372
  43.4 1.3 %copy.9 = bf16[32,32768]{1,0:T(8,128)(2,1)} copy(bf16[32,32768]{1,0:T(8,128)(2,1)S(1)} %bitcast.6) | data formatting | bytes 4194304

commit v7 on v6

--- a/solution.py
+++ b/solution.py
@@ -17,7 +17,7 @@
 
 PEERS = sorted(
     ((dy, dx) for dy in range(4) for dx in range(4) if dy or dx),
-    key=lambda s: -(min(s[0], 4 - s[0]) + min(s[1], 4 - s[1])),
+    key=lambda s: (-min(s[1], 4 - s[1]), -min(s[0], 4 - s[0])),
 )
 UP_TAP = ((1, 2), (None, 0))
 EXT_ORDER = (2, 3, 4, 5, 6, 7, 8, 1, 0, 9, 10, 11)
@@ -93,15 +93,6 @@
     lat_copy(2).start()
     w_copies[2].start()
 
-    def border(p, _):
-        pan[p, 0] = jnp.zeros(pan.shape[2:], F32)
-        pan[p, 65:67] = jnp.zeros((2,) + pan.shape[2:], F32)
-        pan[p, :, 0:8] = jnp.zeros((67, 8, 128), F32)
-        pan[p, :, 72:80] = jnp.zeros((67, 8, 128), F32)
-        return 0
-
-    lax.fori_loop(0, 4, border, 0)
-
     def load_plane(p):
         lat_copy(p).wait()
         pan[p, 1:65, 8:72] = lat[p].astype(F32)
@@ -141,6 +132,15 @@
         )
         for i in range(2)
     ]
+    def border(p, _):
+        pan[p, 0] = jnp.zeros(pan.shape[2:], F32)
+        pan[p, 65:67] = jnp.zeros((2,) + pan.shape[2:], F32)
+        pan[p, :, 0:8] = jnp.zeros((67, 8, 128), F32)
+        pan[p, :, 72:80] = jnp.zeros((67, 8, 128), F32)
+        return 0
+
+    lax.fori_loop(0, 4, border, 0)
+
     load_plane(0)
     gather(0, lambda b: ids[b], reg, 1)
     load_plane(1)

time: 45.1 us -> 45.1 us (level)
  no operation moved by 1% of the time
where the time goes in v7:
time: 45.1 us; the launch traced here: 44.7 us
  Pallas kernels  43.4 us (96%)
  local copies, waits for them, and re-layouts  1.32 us (3%)
    pallas_call x1, Pallas kernels, decode(): pl.pallas_call(kernel, in_specs=[smem, smem, hbm, hbm, hbm, hbm, pl.Block...  43.4 us
    unnamed x1, local copies, waits for them, and re-layouts  1.32 us

profile of v7, /device:TPU:0, one launch (start us, length us, event | category | flops | bytes accessed | tf_op | source)
XLA Modules:
  0.0 44.7 jit_solution(17512502715036218345)
XLA Ops:
  0.0 43.4 %decode.1 = bf16[4,2048,128]{2,1,0:T(8,128)(2,1)S(1)} custom-call(s32[16]{0:T(128)} %ids.1, s32[16]{0:T(128)} %owner.1, bf16[4,64,64,128]{3,2,1,0:T(8,128)(2,1)} %lat_hbm.1, bf16[3,3,3,64,128]{4,3,2,1,0:T(8,128)(2,1)} %bitcast.7, bf16[3,3,3,64,64]{4,3,2,1,0:T(8,128)(2,1)} %w1_hbm.1, bf16[3,3,3,64,64]{4,3,2,1,0:T(8,128)(2,1)} %w2_hbm.1, s32[16,27]{1,0:T(8,128)} %near_ref.1), custom_call_target="tpu_custom_call" | custom-call | tf_op jit(solution)/shard_map/decode/pallas_call | solution.py:372
  43.4 1.3 %copy.9 = bf16[32,32768]{1,0:T(8,128)(2,1)} copy(bf16[32,32768]{1,0:T(8,128)(2,1)S(1)} %bitcast.6) | data formatting | bytes 4194304
